TPU v7x, 512 devices: a whole 4x4x16 slice. The times are simulated.
512 devices in a mesh: seq: 64 (over y, z), head: 8 (over x, core).
Axes of the slice: x: 4, y: 4, z: 16, core: 2. Of those that a mesh axis runs over, the one named last changes fastest.
Arguments:
- mixer_input: bfloat16 [16384, 8192], P('seq', 'head'), may hold values from -6 to 6
- gate_input: bfloat16 [16384, 8192], P('seq', 'head'), may hold values from -5 to 8
- input_map: bfloat16 [16384, 1024], P('seq', 'head'), may hold values from -0.5390625 to 0.5390625
- output_map: bfloat16 [16384, 1024], P('seq', 'head'), may hold values from -0.5390625 to 0.5390625
- step_size: float32 [128, 16384], P('head', 'seq'), may hold values from 0.0125 to 5000, as said below
- decay_rate: float32 [128], P('head'), may hold values from 1e-05 to 0.05
- skip_gain: float32 [128], P('head'), may hold values from 0.2 to 2
- norm_gain: float32 [8192], P('head'), may hold values from 0.25 to 1.75
- queries: bfloat16 [16384, 8192], P('seq', 'head'), may hold values from -200 to 200
- key_rows: bfloat16 [16384, 1024], P('seq', 'head'), may hold values from -6 to 6
- values: bfloat16 [16384, 1024], P('seq', 'head'), may hold values from -6 to 6
- segment: int32 [16384], P('seq'), may hold values from 0 to 15, never falling along the last dimension, each value on 1 to 2048 neighbouring positions
Outputs:
- state_output: bfloat16 [16384, 8192], P('seq', 'head')
- attention_output: bfloat16 [16384, 8192], P('seq', 'head')
Inputs may be any that keep to these rules, and one draw needn't show every extreme that they name: `segment`: segment numbers never fall along the sequence; each document has 1 to 2048 tokens and some document has exactly 2048. `step_size`: positive steps.
All inputs are finite; a program needn't handle non-finite values.
Results may differ from a plain program's by a relative error of at most 0.011.
Values may be sent and summed in bfloat16 or wider, within the bound.
A program may use at most 128 MiB of HBM per device.

v0:
```python
import math

import jax
import jax.numpy as jnp
from jax import lax
from jax.sharding import PartitionSpec as P

SSD_HEADS = 128
HEAD_P = 64
STATE_N = 128
ATT_HEADS = 64
KV_HEADS = 8
HEAD_D = 128
DOC_SPAN = 8


def carried_in(x, axis, join, neutral):
    place = lax.axis_index(axis)
    gathered = jax.tree.map(
        lambda a, kind: lax.all_gather(a.astype(kind), axis),
        x,
        jax.tree.map(lambda a: jnp.bfloat16 if a.dtype == jnp.float32 else a.dtype, x),
    )
    state = jax.tree.map(lambda a, e: jnp.zeros_like(a) + jnp.asarray(e, a.dtype), x, neutral)

    def one(step, state):
        return join(
            state,
            jax.tree.map(
                lambda a, own: lax.dynamic_index_in_dim(a, step, 0, False).astype(own.dtype),
                gathered,
                x,
            ),
        )

    return lax.fori_loop(0, place, one, state)


def shifted(x, axis, by):
    devices = lax.axis_size(axis)
    pairs = [(i, i + by) for i in range(devices) if 0 <= i + by < devices]
    return lax.ppermute(x, axis, pairs)


def chain_combine(earlier, later):
    state_early, total_early, first_early, final_early = earlier
    state_late, total_late, first_late, final_late = later
    joined = (first_late == final_early) | (final_early < 0.0) | (first_late < 0.0)
    carried = jnp.where(joined, total_late, 0.0)
    state_sum = carried[:, None, None] * state_early + state_late
    total_decay = carried * total_early
    first_tag = jnp.where(first_early < 0.0, first_late, first_early)
    final_tag = jnp.where(final_late < 0.0, final_early, final_late)
    return (state_sum, total_decay, first_tag, final_tag)


def attend_group(carried, query_heads, key_block, value_block, allowed):
    row_best, row_total, row_accum = carried
    scores = jnp.einsum(
        "tkrd,ukd->krtu", query_heads, key_block, preferred_element_type=jnp.float32
    ) * (1.0 / math.sqrt(HEAD_D))
    scores = jnp.where(allowed[None, None], scores, -jnp.inf)
    new_best = jnp.maximum(row_best, jnp.max(scores, axis=3))
    shrink = jnp.exp(row_best - new_best)
    weights = jnp.exp(scores - new_best[..., None])
    new_total = row_total * shrink + jnp.sum(weights, axis=3)
    new_accum = row_accum * shrink[..., None] + jnp.einsum(
        "krtu,ukd->krtd",
        weights.astype(jnp.bfloat16),
        value_block,
        preferred_element_type=jnp.float32,
    )
    return (new_best, new_total, new_accum)


def per_device(
    mixer_input,
    gate_input,
    input_map,
    output_map,
    step_size,
    decay_rate,
    skip_gain,
    norm_gain,
    queries,
    key_rows,
    values,
    segment,
):
    row_count = mixer_input.shape[0]
    head_count = step_size.shape[0]
    group_count = input_map.shape[1] // STATE_N
    repeat_count = head_count // group_count
    mixer_heads = mixer_input.reshape(row_count, head_count, HEAD_P).transpose(1, 0, 2)
    in_groups = input_map.reshape(row_count, group_count, STATE_N).transpose(1, 0, 2)
    out_groups = output_map.reshape(row_count, group_count, STATE_N).transpose(1, 0, 2)
    seg_float = segment.astype(jnp.float32)
    cumulative = jnp.cumsum(step_size * decay_rate[:, None], axis=1)
    position = jnp.arange(row_count, dtype=jnp.int32)
    allowed_local = (segment[:, None] == segment[None, :]) & (
        position[None, :] <= position[:, None]
    )
    spread_gap = cumulative[:, :, None] - cumulative[:, None, :]
    decay_grid = jnp.where(
        allowed_local[None], jnp.exp(-jnp.where(allowed_local[None], spread_gap, 0.0)), 0.0
    )
    inner_group = lax.dot_general(
        out_groups, in_groups, (((2,), (2,)), ((0,), (0,))), preferred_element_type=jnp.float32
    )
    inner_head = jnp.repeat(inner_group, repeat_count, axis=0)
    mixing = (decay_grid * inner_head).astype(jnp.bfloat16)
    intra = lax.dot_general(
        mixing, mixer_heads, (((2,), (1,)), ((0,), (0,))), preferred_element_type=jnp.float32
    )
    last_cum = cumulative[:, -1]
    tail = jnp.where(
        segment[None, :] == segment[-1], jnp.exp(-(last_cum[:, None] - cumulative)), 0.0
    )
    in_heads = jnp.repeat(in_groups, repeat_count, axis=0)
    scaled = (tail[:, :, None] * in_heads).astype(jnp.bfloat16)
    block_state = lax.dot_general(
        mixer_heads, scaled, (((1,), (1,)), ((0,), (0,))), preferred_element_type=jnp.float32
    )
    total_decay = jnp.exp(-last_cum) * (segment[0] == segment[-1]).astype(jnp.float32)
    element = (block_state, total_decay, seg_float[0], seg_float[-1])
    identity = (
        jnp.zeros_like(block_state),
        jnp.ones_like(total_decay),
        jnp.float32(-1.0),
        jnp.float32(-1.0),
    )
    prefix = carried_in(element, "seq", chain_combine, identity)
    state_in, prefix_decay, prefix_first, prefix_final = prefix
    enter = jnp.where(seg_float[None, :] == prefix_final, jnp.exp(-cumulative), 0.0)
    out_heads = jnp.repeat(out_groups, repeat_count, axis=0).astype(jnp.float32)
    incoming = lax.dot_general(
        out_heads,
        state_in,
        (((2,), (2,)), ((0,), (0,))),
        precision=lax.Precision.HIGHEST,
        preferred_element_type=jnp.float32,
    )
    mixed = (
        intra
        + enter[:, :, None] * incoming
        + skip_gain[:, None, None] * mixer_heads.astype(jnp.float32)
    )
    gate_heads = (
        gate_input.reshape(row_count, head_count, HEAD_P).transpose(1, 0, 2).astype(jnp.float32)
    )
    gated = mixed * jax.nn.silu(gate_heads)
    squares_local = jnp.sum(gated * gated, axis=(0, 2))
    squares_all = lax.psum(squares_local, "head")
    row_scale = lax.rsqrt(squares_all / (SSD_HEADS * HEAD_P) + 1e-05)
    normed = gated * row_scale[None, :, None] * norm_gain.reshape(head_count, 1, HEAD_P)
    state_output = (
        normed.transpose(1, 0, 2).reshape(row_count, head_count * HEAD_P).astype(jnp.bfloat16)
    )
    kv_local = key_rows.shape[1] // HEAD_D
    group_size = ATT_HEADS // KV_HEADS
    query_heads = queries.reshape(row_count, kv_local, group_size, HEAD_D)
    seq_index = lax.axis_index("seq")
    seg_half = segment.astype(jnp.bfloat16)
    query_pos = seq_index * row_count + position
    moving = (key_rows, values, seg_half)
    collected = [moving]
    for hop_index in range(DOC_SPAN):
        moving = shifted((moving[0], moving[1], moving[2]), "seq", 1)
        collected.append(moving)
    carried = (
        jnp.full((kv_local, group_size, row_count), -jnp.inf, jnp.float32),
        jnp.zeros((kv_local, group_size, row_count), jnp.float32),
        jnp.zeros((kv_local, group_size, row_count, HEAD_D), jnp.float32),
    )
    for first_block in range(0, len(collected), 3):
        members = collected[first_block : first_block + 3]
        key_block = jnp.concatenate([member[0] for member in members], axis=0).reshape(
            -1, kv_local, HEAD_D
        )
        value_block = jnp.concatenate([member[1] for member in members], axis=0).reshape(
            -1, kv_local, HEAD_D
        )
        key_seg = jnp.concatenate([member[2] for member in members], axis=0)
        key_pos = jnp.concatenate(
            [
                (seq_index - (first_block + offset)) * row_count + position
                for offset in range(len(members))
            ],
            axis=0,
        )
        key_valid = jnp.concatenate(
            [
                jnp.broadcast_to(seq_index >= first_block + offset, (row_count,))
                for offset in range(len(members))
            ],
            axis=0,
        )
        allowed = (
            (key_pos[None, :] <= query_pos[:, None])
            & key_valid[None, :]
            & (key_seg[None, :] == seg_half[:, None])
        )

        def attend_here(state_now, key_block=key_block, value_block=value_block, allowed=allowed):
            return attend_group(state_now, query_heads, key_block, value_block, allowed)

        carried = attend_here(carried)
    row_best, row_total, row_accum = carried
    attended = row_accum / row_total[..., None]
    attention_output = (
        attended.transpose(2, 0, 1, 3)
        .reshape(row_count, kv_local * group_size * HEAD_D)
        .astype(jnp.bfloat16)
    )
    return (state_output, attention_output)


def solution(mesh):
    in_specs = (
        P("seq", "head"),
        P("seq", "head"),
        P("seq", "head"),
        P("seq", "head"),
        P("head", "seq"),
        P("head"),
        P("head"),
        P("head"),
        P("seq", "head"),
        P("seq", "head"),
        P("seq", "head"),
        P("seq"),
    )
    out_specs = (P("seq", "head"), P("seq", "head"))
    return jax.shard_map(
        per_device, mesh=mesh, in_specs=in_specs, out_specs=out_specs, check_vma=False
    )
```

profile of v0, /device:TPU:505, one launch (start us, length us, event | category | flops | bytes accessed | tf_op | source)
XLA Modules:
  0.0 618.7 jit_solution(12765884722748234616)
XLA Ops:
  14.0 1.5 fusion.43
  22.8 1.5 fusion.69
  27.2 5.3 collective-permute-done.1
  33.9 3.3 collective-permute-done.6
  39.8 2.0 collective-permute-done.7
  48.5 114.0 %all-reduce.3 = (bf16[64]{0:T(256)(128)(2,1)S(1)}, bf16[1024]{0:T(1024)(128)(2,1)S(1)}, bf16[64]{0:T(256)(128)(2,1)S(1)}) all-reduce(bf16[64]{0:T(256)(128)(2,1)S(1)} %dynamic-update-slice, bf16[1024]{0:T(1024)(128)(2,1)S(1)} %dynamic-update-slice.1, bf16[64]{0:T(256)(128)(2,1)S(1)} %dynamic-update-slice.2), channel_id=1, replica_groups=mesh['seq'=64,'head'=8] {'seq'}, use_global_device_ids=true, to_apply=%add | all-reduce | flops 1152 | bytes 4608
  167.2 2.1 collective-permute-done.16
  171.9 1.5 collective-permute-done.3
  174.7 3.4 collective-permute-done.5
  181.5 3.4 collective-permute-done.12
  189.6 2.1 collective-permute-done.13
  195.1 1.9 fusion.7
  197.0 1.9 collective-permute-done.14
  203.5 3.8 collective-permute-done.21
  211.8 1.9 collective-permute-done.22
  213.7 1.5 collective-permute-start.23
  219.5 1.8 fusion.40
  221.3 1.8 fusion.34
  223.1 1.8 divide_convert_fusion
  225.9 332.7 %while.15 = (s32[]{:T(128)}, f32[16,64,128]{2,1,0:T(8,128)S(1)}, f32[]{:T(128)}, s32[]{:T(128)}, bf16[64]{0:T(256)(128)(2,1)S(1)}, /*index=5*/bf16[64,16]{1,0:T(...) while((s32[]{:T(128)}, f32[16,64,128]{2,1,0:T(8,128)S(1)}, ...), condition=%wide.region_3.4_spmd, body=%wide.region_2.3_spmd.sunk | while | flops 393260 | bytes 1311103 | solution.py:36
  560.0 3.9 fusion.47
  563.9 43.4 %psum.7 = f32[256]{0:T(256)S(1)} all-reduce(f32[256]{0:T(256)S(1)} %get-tuple-element.116), channel_id=1, replica_groups=mesh['seq'=64,'head'=8] {'head'}, use_global_device_ids=true, to_apply=%region_5.6 | all-reduce | flops 256 | bytes 2048 | tf_op jit(solution)/shard_map/psum | solution.py:153
  607.3 2.5 fusion.53
  609.8 2.0 copy.72
  (368 shorter events, 216.3 us)
Async XLA Ops:
  7.2 218.7 %all-gather.4.cloned.1.call-start = ((), (), s32[]{:S(2)}) async-start(), calls=%async_computation | async-start | bytes 17039360 | tf_op jit(solution)/shard_map/all_gather | solution.py:20
  16.3 9.6 %collective-permute-start = (bf16[256]{0:T(256)(128)(2,1)S(1)}, bf16[256]{0:T(256)(128)(2,1)S(1)}, u32[]{:S(2)}, u32[]{:S(2)}) collective-permute-start(bf16[256]{0:T(256)(128)(2,1)S(1)} %get-tuple-element.110), channel_id=1, source_target_pairs={{0,8},{8,16},{16,24},{24,32},{32,40},{40,48},{48,56},{56,64},{64,7... | collective-permute-start | bytes 1544 | tf_op jit(solution)/shard_map/ppermute | solution.py:42
  17.6 148.3 %collective-permute-start.2 = (bf16[256,128]{1,0:T(8,128)(2,1)}, bf16[256,128]{1,0:T(8,128)(2,1)S(1)}, u32[]{:S(2)}, u32[]{:S(2)}) collective-permute-start(bf16[256,128]{1,0:T(8,128)(2,1)} %param.23), channel_id=1, source_target_pairs={{0,8},{8,16},{16,24},{24,32},{32,40},{40,48},{48,56},{56,64},{64,7... | collective-permute-start | bytes 196616 | tf_op jit(solution)/shard_map/ppermute | solution.py:42
  19.9 150.7 %collective-permute-start.4 = (bf16[256,128]{0,1:T(8,128)(2,1)S(1)}, bf16[256,128]{0,1:T(8,128)(2,1)S(1)}, u32[]{:S(2)}, u32[]{:S(2)}) collective-permute-start(bf16[256,128]{0,1:T(8,128)(2,1)S(1)} %copy.66), channel_id=1, source_target_pairs={{0,8},{8,16},{16,24},{24,32},{32,40},{40,48},{48,56},{56,64},{64,7... | collective-permute-start | bytes 196616 | tf_op jit(solution)/shard_map/ppermute | solution.py:42
  25.9 6.6 %collective-permute-start.1 = (bf16[256]{0:T(256)(128)(2,1)S(1)}, bf16[256]{0:T(256)(128)(2,1)S(1)}, u32[]{:S(2)}, u32[]{:S(2)}) collective-permute-start(bf16[256]{0:T(256)(128)(2,1)S(1)} %collective-permute-done), channel_id=1, source_target_pairs={{0,8},{8,16},{16,24},{24,32},{32,40},{40,48},{48,56},{56,64},{64,7... | collective-permute-start | bytes 1544 | tf_op jit(solution)/shard_map/ppermute | solution.py:42
  32.5 4.7 collective-permute-start.6
  37.1 4.7 collective-permute-start.7
  41.8 5.1 collective-permute-start.8
  46.9 117.7 %collective-permute-start.15 = (bf16[256]{0:T(256)(128)(2,1)S(1)}, bf16[256]{0:T(256)(128)(2,1)S(1)}, u32[]{:S(2)}, u32[]{:S(2)}) collective-permute-start(bf16[256]{0:T(256)(128)(2,1)S(1)} %collective-permute-done.8), channel_id=1, source_target_pairs={{0,8},{8,16},{16,24},{24,32},{32,40},{40,48},{48,56},{56,64},{64,7... | collective-permute-start | bytes 1544 | tf_op jit(solution)/shard_map/ppermute | solution.py:42
  165.9 7.5 %collective-permute-start.3 = (bf16[256,128]{1,0:T(8,128)(2,1)S(1)}, bf16[256,128]{1,0:T(8,128)(2,1)S(1)}, u32[]{:S(2)}, u32[]{:S(2)}) collective-permute-start(bf16[256,128]{1,0:T(8,128)(2,1)S(1)} %collective-permute-done.2), channel_id=1, source_target_pairs={{0,8},{8,16},{16,24},{24,32},{32,40},{40,48},{48,56},{56,64},{64,7... | collective-permute-start | bytes 196616 | tf_op jit(solution)/shard_map/ppermute | solution.py:42
  169.3 12.1 %collective-permute-start.17 = (bf16[256]{0:T(256)(128)(2,1)S(1)}, bf16[256]{0:T(256)(128)(2,1)S(1)}, u32[]{:S(2)}, u32[]{:S(2)}) collective-permute-start(bf16[256]{0:T(256)(128)(2,1)S(1)} %collective-permute-done.16), channel_id=1, source_target_pairs={{0,8},{8,16},{16,24},{24,32},{32,40},{40,48},{48,56},{56,64},{64,7... | collective-permute-start | bytes 1544 | tf_op jit(solution)/shard_map/ppermute | solution.py:42
  170.6 7.5 %collective-permute-start.5 = (bf16[256,128]{0,1:T(8,128)(2,1)S(1)}, bf16[256,128]{0,1:T(8,128)(2,1)S(1)}, u32[]{:S(2)}, u32[]{:S(2)}) collective-permute-start(bf16[256,128]{0,1:T(8,128)(2,1)S(1)} %collective-permute-done.4), channel_id=1, source_target_pairs={{0,8},{8,16},{16,24},{24,32},{32,40},{40,48},{48,56},{56,64},{64,7... | collective-permute-start | bytes 196616 | tf_op jit(solution)/shard_map/ppermute | solution.py:42
  173.4 6.8 %collective-permute-start.9 = (bf16[256,128]{1,0:T(8,128)(2,1)S(1)}, bf16[256,128]{1,0:T(8,128)(2,1)S(1)}, u32[]{:S(2)}, u32[]{:S(2)}) collective-permute-start(bf16[256,128]{1,0:T(8,128)(2,1)S(1)} %collective-permute-done.3), channel_id=1, source_target_pairs={{0,8},{8,16},{16,24},{24,32},{32,40},{40,48},{48,56},{56,64},{64,7... | collective-permute-start | bytes 196616 | tf_op jit(solution)/shard_map/ppermute | solution.py:42
  178.0 6.8 %collective-permute-start.12 = (bf16[256,128]{0,1:T(8,128)(2,1)S(1)}, bf16[256,128]{0,1:T(8,128)(2,1)S(1)}, u32[]{:S(2)}, u32[]{:S(2)}) collective-permute-start(bf16[256,128]{0,1:T(8,128)(2,1)S(1)} %collective-permute-done.5), channel_id=1, source_target_pairs={{0,8},{8,16},{16,24},{24,32},{32,40},{40,48},{48,56},{56,64},{64,7... | collective-permute-start | bytes 196616 | tf_op jit(solution)/shard_map/ppermute | solution.py:42
  180.1 6.8 %collective-permute-start.10 = (bf16[256,128]{1,0:T(8,128)(2,1)S(1)}, bf16[256,128]{1,0:T(8,128)(2,1)S(1)}, u32[]{:S(2)}, u32[]{:S(2)}) collective-permute-start(bf16[256,128]{1,0:T(8,128)(2,1)S(1)} %collective-permute-done.9), channel_id=1, source_target_pairs={{0,8},{8,16},{16,24},{24,32},{32,40},{40,48},{48,56},{56,64},{64,7... | collective-permute-start | bytes 196616 | tf_op jit(solution)/shard_map/ppermute | solution.py:42
  184.8 6.8 %collective-permute-start.13 = (bf16[256,128]{0,1:T(8,128)(2,1)S(1)}, bf16[256,128]{0,1:T(8,128)(2,1)S(1)}, u32[]{:S(2)}, u32[]{:S(2)}) collective-permute-start(bf16[256,128]{0,1:T(8,128)(2,1)S(1)} %collective-permute-done.12), channel_id=1, source_target_pairs={{0,8},{8,16},{16,24},{24,32},{32,40},{40,48},{48,56},{56,64},{64,7... | collective-permute-start | bytes 196616 | tf_op jit(solution)/shard_map/ppermute | solution.py:42
  187.0 6.8 %collective-permute-start.11 = (bf16[256,128]{1,0:T(8,128)(2,1)S(1)}, bf16[256,128]{1,0:T(8,128)(2,1)S(1)}, u32[]{:S(2)}, u32[]{:S(2)}) collective-permute-start(bf16[256,128]{1,0:T(8,128)(2,1)S(1)} %collective-permute-done.10), channel_id=1, source_target_pairs={{0,8},{8,16},{16,24},{24,32},{32,40},{40,48},{48,56},{56,64},{64,7... | collective-permute-start | bytes 196616 | tf_op jit(solution)/shard_map/ppermute | solution.py:42
  191.6 7.2 %collective-permute-start.14 = (bf16[256,128]{0,1:T(8,128)(2,1)S(1)}, bf16[256,128]{0,1:T(8,128)(2,1)S(1)}, u32[]{:S(2)}, u32[]{:S(2)}) collective-permute-start(bf16[256,128]{0,1:T(8,128)(2,1)S(1)} %collective-permute-done.13), channel_id=1, source_target_pairs={{0,8},{8,16},{16,24},{24,32},{32,40},{40,48},{48,56},{56,64},{64,7... | collective-permute-start | bytes 196616 | tf_op jit(solution)/shard_map/ppermute | solution.py:42
  193.8 7.2 %collective-permute-start.18 = (bf16[256,128]{1,0:T(8,128)(2,1)S(1)}, bf16[256,128]{1,0:T(8,128)(2,1)S(1)}, u32[]{:S(2)}, u32[]{:S(2)}) collective-permute-start(bf16[256,128]{1,0:T(8,128)(2,1)S(1)} %collective-permute-done.11), channel_id=1, source_target_pairs={{0,8},{8,16},{16,24},{24,32},{32,40},{40,48},{48,56},{56,64},{64,7... | collective-permute-start | bytes 196616 | tf_op jit(solution)/shard_map/ppermute | solution.py:42
  198.8 8.5 %collective-permute-start.21 = (bf16[256,128]{0,1:T(8,128)(2,1)S(1)}, bf16[256,128]{0,1:T(8,128)(2,1)S(1)}, u32[]{:S(2)}, u32[]{:S(2)}) collective-permute-start(bf16[256,128]{0,1:T(8,128)(2,1)S(1)} %collective-permute-done.14), channel_id=1, source_target_pairs={{0,8},{8,16},{16,24},{24,32},{32,40},{40,48},{48,56},{56,64},{64,7... | collective-permute-start | bytes 196616 | tf_op jit(solution)/shard_map/ppermute | solution.py:42
  200.9 8.5 %collective-permute-start.19 = (bf16[256,128]{1,0:T(8,128)(2,1)S(1)}, bf16[256,128]{1,0:T(8,128)(2,1)S(1)}, u32[]{:S(2)}, u32[]{:S(2)}) collective-permute-start(bf16[256,128]{1,0:T(8,128)(2,1)S(1)} %collective-permute-done.18), channel_id=1, source_target_pairs={{0,8},{8,16},{16,24},{24,32},{32,40},{40,48},{48,56},{56,64},{64,7... | collective-permute-start | bytes 196616 | tf_op jit(solution)/shard_map/ppermute | solution.py:42
  207.3 6.4 %collective-permute-start.22 = (bf16[256,128]{0,1:T(8,128)(2,1)S(1)}, bf16[256,128]{0,1:T(8,128)(2,1)S(1)}, u32[]{:S(2)}, u32[]{:S(2)}) collective-permute-start(bf16[256,128]{0,1:T(8,128)(2,1)S(1)} %collective-permute-done.21), channel_id=1, source_target_pairs={{0,8},{8,16},{16,24},{24,32},{32,40},{40,48},{48,56},{56,64},{64,7... | collective-permute-start | bytes 196616 | tf_op jit(solution)/shard_map/ppermute | solution.py:42
  209.4 6.3 %collective-permute-start.20 = (bf16[256,128]{1,0:T(8,128)(2,1)S(1)}, bf16[256,128]{1,0:T(8,128)(2,1)S(1)}, u32[]{:S(2)}, u32[]{:S(2)}) collective-permute-start(bf16[256,128]{1,0:T(8,128)(2,1)S(1)} %collective-permute-done.19), channel_id=1, source_target_pairs={{0,8},{8,16},{16,24},{24,32},{32,40},{40,48},{48,56},{56,64},{64,7... | collective-permute-start | bytes 196616 | tf_op jit(solution)/shard_map/ppermute | solution.py:42
  213.7 9.4 %collective-permute-start.23 = (bf16[256,128]{0,1:T(8,128)(2,1)S(1)}, bf16[256,128]{0,1:T(8,128)(2,1)S(1)}, u32[]{:S(2)}, u32[]{:S(2)}) collective-permute-start(bf16[256,128]{0,1:T(8,128)(2,1)S(1)} %collective-permute-done.22), channel_id=1, source_target_pairs={{0,8},{8,16},{16,24},{24,32},{32,40},{40,48},{48,56},{56,64},{64,7... | collective-permute-start | bytes 196616 | tf_op jit(solution)/shard_map/ppermute | solution.py:42
  (7 other events, 1392.3 us)
Sparse Core Ops, SparseCore 0:
  15.7 197.4 all-gather.3
where the time goes:
time: 624 us; the launch traced here: 619 us
  loops' own time  178 us (29%)
  blocking collectives  157 us (25%)
  local copies, waits for them, and re-layouts  98 us (16%)
  other arithmetic  85.2 us (14%)
  waiting for transfers between devices  35.7 us (6%)
  starting transfers between devices  31 us (5%)
  matrix products  17 us (3%)
  between operations  16.6 us (3%)
    another operation x1, loops' own time, carried_in(): return lax.fori_loop(0, place, one, state)  178 us
    unnamed x1, blocking collectives  114 us
    dynamic_slice x126, local copies, waits for them, and re-layouts, one(): lax.dynamic_index_in_dim(a, step, 0, False).astype(own.dtype)  84 us
    add x63, other arithmetic, chain_combine(): state_sum = carried[:, None, None] * state_early + state_late  70 us
    psum x1, blocking collectives, per_device(): squares_all = lax.psum(squares_local, 'head')  43.4 us
    ppermute x24, waiting for transfers between devices, shifted(): return lax.ppermute(x, axis, pairs)  35.7 us
    ppermute x24, starting transfers between devices, shifted(): return lax.ppermute(x, axis, pairs)  31 us
  transfers between devices with their start and end apart: 25, of which 18 were waited for; matrix products, arithmetic and copies ran while one was open for 4% of the time, Pallas kernels for 0%

commit v1 on v0

v1 whole, which is shorter than its diff:
```python
import math

import jax
import jax.numpy as jnp
from jax import lax
from jax.experimental import pallas as pl
from jax.experimental.pallas import tpu as pltpu
from jax.sharding import PartitionSpec as P

SSD_HEADS = 128
HEAD_P = 64
STATE_N = 128
ATT_HEADS = 64
HEAD_D = 128
DOC_SPAN = 8
TOKENS = 256
N_SEQ = 64
RING = 16
N_HEAD = 8
LOCAL_HEADS = SSD_HEADS // N_HEAD
LOCAL_ATT = ATT_HEADS // N_HEAD
PAIRS = LOCAL_HEADS // 2
KT_ROWS = HEAD_D + 16
MSG = HEAD_P + 16
LOG2E = 1.0 / math.log(2.0)
SCORE_SCALE = LOG2E / math.sqrt(HEAD_D)
FAR = float(2**19)
MESH = pl.DeviceIdType.MESH
F32 = jnp.float32
BF16 = jnp.bfloat16


def dot(a, b, contract=((1,), (0,))):
    return lax.dot_general(a, b, (contract, ((), ())), preferred_element_type=F32)


def kernel(
    x_ref, gate_ref, in_ref, out_ref, step_ref, decay_ref, skip_ref, gain_ref, q_ref, k_ref, v_ref, seg_ref,
    state_ref, att_ref,
    kt_buf, v_buf, send_buf, scan_buf, local_buf, back_buf, carry_buf, in_buf, sq_buf,
    y_buf, acc_buf, max_buf, g_buf, onehot_buf, col_buf, cum_buf,
    kt_send, kt_recv, v_send, v_recv, a_send, a_recv, c_send, c_recv, b_send, b_recv, s_send, s_recv,
):
    me = lax.axis_index("seq")
    head = lax.axis_index("head")
    row, z = me // RING, me % RING
    succ, pred = (me + 1) % N_SEQ, (me + N_SEQ - 1) % N_SEQ
    below, above = (me + RING) % N_SEQ, (me + N_SEQ - RING) % N_SEQ

    def ring(d):
        return row * RING + (z + d) % RING

    barrier = pltpu.get_barrier_semaphore()
    for d in sorted(range(1, RING), key=lambda d: -min(d, RING - d)):
        pl.semaphore_signal(barrier, inc=1, device_id={"seq": ring(d)}, device_id_type=MESH)
    for other in (below, above, succ, pred):
        pl.semaphore_signal(barrier, inc=1, device_id={"seq": other}, device_id_type=MESH)
    for d in range(1, N_HEAD):
        pl.semaphore_signal(barrier, inc=1, device_id={"head": (head + d) % N_HEAD}, device_id_type=MESH)

    def kv_copies(hop):
        return (
            pltpu.make_async_remote_copy(
                src_ref=kt_buf.at[hop, pl.ds(0, KT_ROWS)],
                dst_ref=kt_buf.at[hop + 1, pl.ds(0, KT_ROWS)],
                send_sem=kt_send.at[hop],
                recv_sem=kt_recv.at[hop],
                device_id={"seq": succ},
                device_id_type=MESH,
            ),
            pltpu.make_async_remote_copy(
                src_ref=v_buf.at[hop],
                dst_ref=v_buf.at[hop + 1],
                send_sem=v_send.at[hop],
                recv_sem=v_recv.at[hop],
                device_id={"seq": succ},
                device_id_type=MESH,
            ),
        )

    def scan_copy(d):
        return pltpu.make_async_remote_copy(
            src_ref=send_buf.at[(z + d) % RING],
            dst_ref=scan_buf.at[z],
            send_sem=a_send.at[d],
            recv_sem=a_recv.at[d],
            device_id={"seq": ring(d)},
            device_id_type=MESH,
        )

    def back_copy(d):
        return pltpu.make_async_remote_copy(
            src_ref=back_buf.at[(z + d) % RING],
            dst_ref=in_buf.at[z],
            send_sem=b_send.at[d],
            recv_sem=b_recv.at[d],
            device_id={"seq": ring(d)},
            device_id_type=MESH,
        )

    def square_copy(d):
        return pltpu.make_async_remote_copy(
            src_ref=sq_buf.at[head],
            dst_ref=sq_buf.at[head],
            send_sem=s_send.at[d],
            recv_sem=s_recv.at[d],
            device_id={"head": (head + d) % N_HEAD},
            device_id_type=MESH,
        )

    carry_copy = pltpu.make_async_remote_copy(
        src_ref=carry_buf.at[0],
        dst_ref=carry_buf.at[1],
        send_sem=c_send.at[0],
        recv_sem=c_recv.at[0],
        device_id={"seq": below},
        device_id_type=MESH,
    )
    far_first = sorted(range(1, RING), key=lambda d: -min(d, RING - d))

    lane = lax.broadcasted_iota(jnp.int32, (LOCAL_HEADS, TOKENS), 1)
    diagonal = lax.broadcasted_iota(jnp.int32, (LOCAL_HEADS, LOCAL_HEADS), 0) == lax.broadcasted_iota(
        jnp.int32, (LOCAL_HEADS, LOCAL_HEADS), 1
    )
    rate = jnp.sum(
        jnp.where(diagonal, jnp.broadcast_to(decay_ref[...], (LOCAL_HEADS, LOCAL_HEADS)), 0.0), axis=1, keepdims=True
    )
    cum = step_ref[...] * rate
    reach = 1
    while reach < TOKENS:
        cum = cum + jnp.where(lane >= reach, pltpu.roll(cum, reach, 1), 0.0)
        reach *= 2
    cum = cum * LOG2E
    cum_buf[...] = cum
    seg_row = seg_ref[...].astype(F32)
    seg_last = seg_row[:, TOKENS - 1 :]
    seg_first = seg_row[:, :1]
    last_cum = cum[:, TOKENS - 1 :]
    tail = jnp.where(seg_row == seg_last, jnp.exp2(jnp.minimum(cum - last_cum, 0.0)), 0.0)
    enter = jnp.where(seg_row == seg_first, jnp.exp2(-cum), 0.0)
    col_buf[...] = jnp.concatenate(
        [cum, tail, enter, jnp.zeros((128 - 3 * LOCAL_HEADS, TOKENS), F32)], axis=0
    ).T
    in_map = in_ref[...]
    in_map_t = in_map.astype(F32).T.astype(BF16)
    first_half = lax.broadcasted_iota(jnp.int32, (TOKENS, 128), 1) < HEAD_P

    def pair_columns(base, p):
        a = jnp.broadcast_to(col_buf[:, base + 2 * p : base + 2 * p + 1], (TOKENS, 128))
        b = jnp.broadcast_to(col_buf[:, base + 2 * p + 1 : base + 2 * p + 2], (TOKENS, 128))
        return jnp.where(first_half, a, b)

    block_decay = jnp.broadcast_to(jnp.exp2(-last_cum), (LOCAL_HEADS, 128))
    decay_hi = block_decay.astype(BF16).astype(F32)
    decay_lo = block_decay - decay_hi
    note_row = lax.broadcasted_iota(jnp.int32, (16, 128), 0)
    tags = jnp.where(
        note_row == 2,
        jnp.broadcast_to(seg_first, (16, 128)),
        jnp.where(note_row == 3, jnp.broadcast_to(seg_last, (16, 128)), 0.0),
    )
    for p in range(PAIRS):
        weighted = (x_ref[:, p * 128 : (p + 1) * 128].astype(F32) * pair_columns(LOCAL_HEADS, p)).astype(BF16)
        end_state = dot(in_map_t, weighted).T.astype(BF16)
        for half in range(2):
            h = 2 * p + half
            send_buf[h, :HEAD_P] = end_state[half * HEAD_P : (half + 1) * HEAD_P]
            note = jnp.where(
                note_row == 0,
                jnp.broadcast_to(decay_hi[h : h + 1], (16, 128)),
                jnp.where(note_row == 1, jnp.broadcast_to(decay_lo[h : h + 1], (16, 128)), tags),
            )
            send_buf[h, HEAD_P:] = note.astype(BF16)

    kt_buf[0, :HEAD_D] = k_ref[...].astype(F32).T.astype(BF16)
    documents = lax.broadcasted_iota(jnp.int32, (16, TOKENS), 0).astype(F32)
    kt_buf[0, HEAD_D:KT_ROWS] = jnp.where(documents == seg_row, 0.0, -FAR).astype(BF16)
    v_buf[0] = v_ref[...]
    for hop in range(DOC_SPAN + 1):
        kt_buf[hop, KT_ROWS:] = jnp.zeros((TOKENS - KT_ROWS, TOKENS), BF16)

    pl.semaphore_wait(barrier, RING - 1 + 4 + N_HEAD - 1)
    for d in far_first:
        scan_copy(d).start()
    for copy in kv_copies(0):
        copy.start()
    scan_buf[z] = send_buf[z]

    def forward(hop):
        for copy, onward in zip(kv_copies(hop - 1), kv_copies(hop) if hop < DOC_SPAN else (None, None)):
            copy.wait_recv()
            if onward is not None:
                onward.start()

    seg_col = jnp.broadcast_to(seg_row, (128, TOKENS)).T
    onehot_buf[...] = jnp.where(
        lax.broadcasted_iota(jnp.int32, (TOKENS, 128), 1).astype(F32) == seg_col, 1.0, 0.0
    ).astype(BF16)
    causal = lax.broadcasted_iota(jnp.int32, (TOKENS, TOKENS), 1) <= lax.broadcasted_iota(
        jnp.int32, (TOKENS, TOKENS), 0
    )
    same = jnp.concatenate([seg_col, seg_col], axis=1) == jnp.broadcast_to(seg_row, (TOKENS, TOKENS))
    g_buf[...] = jnp.where(causal & same, dot(out_ref[...], in_map, ((1,), (1,))), 0.0)

    def within(pairs):
        for p in pairs:
            x_pair = x_ref[:, p * 128 : (p + 1) * 128]
            zero = jnp.zeros_like(x_pair)
            total = jnp.zeros((TOKENS, 128), F32)
            for half in range(2):
                h = 2 * p + half
                gap = jnp.broadcast_to(cum_buf[h : h + 1, :], (TOKENS, TOKENS)) - jnp.broadcast_to(
                    col_buf[:, h : h + 1], (TOKENS, TOKENS)
                )
                mixing = (jnp.exp2(jnp.minimum(gap, 0.0)) * g_buf[...]).astype(BF16)
                x_half = jnp.where(first_half, x_pair, zero) if half == 0 else jnp.where(first_half, zero, x_pair)
                total = total + dot(mixing, x_half)
            skip = jnp.where(
                first_half[:1], skip_ref[:, 2 * p : 2 * p + 1], skip_ref[:, 2 * p + 1 : 2 * p + 2]
            )
            y_buf[p] = total + skip * x_pair.astype(F32)

    def attend(hops):
        first, final = hops[0] == 0, hops[-1] == DOC_SPAN

        def one(h, _):
            columns = pl.ds(pl.multiple_of(h * HEAD_D, HEAD_D), HEAD_D)
            q = jnp.concatenate([q_ref[:, columns], onehot_buf[...]], axis=1)
            scores = []
            for hop in hops:
                s = dot(q, kt_buf[hop])
                if hop == 0:
                    s = jnp.where(causal, s, -2.0 * FAR)
                scores.append(s)
            top = scores[0]
            for s in scores[1:]:
                top = jnp.maximum(top, s)
            best = jnp.broadcast_to(jnp.max(top, axis=1, keepdims=True), (TOKENS, 128))
            if not first:
                before = max_buf[h]
                best = jnp.maximum(before, best)
            best2 = jnp.concatenate([best, best], axis=1)
            ones = jnp.ones((TOKENS, HEAD_D), BF16)
            total = None
            for hop, s in zip(hops, scores):
                weights = jnp.exp2((s - best2) * SCORE_SCALE).astype(BF16)
                part = dot(weights, jnp.concatenate([v_buf[hop], ones], axis=1))
                total = part if total is None else total + part
            if not first:
                shrink = jnp.exp2((before - best) * SCORE_SCALE)
                total = total + acc_buf[h] * jnp.concatenate([shrink, shrink], axis=1)
            if final:
                att_ref[:, columns] = (total[:, :HEAD_D] / total[:, HEAD_D:]).astype(BF16)
            else:
                acc_buf[h] = total
                max_buf[h] = best
            return 0

        lax.fori_loop(0, LOCAL_ATT, one, 0)

    within(range(0, 4))
    forward(1)
    within(range(4, 8))
    forward(2)
    attend((0,))
    forward(3)
    attend((1, 2))

    for d in far_first:
        scan_copy(d).wait_recv()
    state = jnp.zeros((HEAD_P, STATE_N), F32)
    product = jnp.ones((1, STATE_N), F32)
    notes = []
    last_before = None
    for i in range(RING):
        block = scan_buf[i].astype(F32)
        decay = block[HEAD_P : HEAD_P + 1] + block[HEAD_P + 1 : HEAD_P + 2]
        tag_first, tag_last = block[HEAD_P + 2 : HEAD_P + 3], block[HEAD_P + 3 : HEAD_P + 4]
        if i >= DOC_SPAN:
            back_buf[i] = jnp.where(tag_first == last_before, state, 0.0).astype(BF16)
        else:
            local_buf[i] = state
            notes.append((product, tag_first, last_before))
        kept = decay if i == 0 else jnp.where(tag_last == last_before, decay, 0.0)
        state = block[:HEAD_P] + kept * state
        product = product * decay
        last_before = tag_last
    carry_buf[0, :HEAD_P] = state.astype(BF16)
    carry_buf[0, HEAD_P:] = jnp.broadcast_to(last_before, (16, STATE_N)).astype(BF16)
    carry_copy.start()
    for d in far_first:

        @pl.when((z + d) % RING >= DOC_SPAN)
        def _(d=d):
            back_copy(d).start()

    forward(4)
    carry_copy.wait_recv()
    carried = carry_buf[1, :HEAD_P].astype(F32)
    carried_tag = carry_buf[1, HEAD_P:].astype(F32)[:1]
    for i, (product, tag_first, last_before) in enumerate(notes):
        if i == 0:
            full = jnp.where(tag_first == carried_tag, carried, 0.0)
        else:
            full = local_buf[i] + jnp.where(carried_tag == last_before, product, 0.0) * carried
            full = jnp.where(tag_first == last_before, full, 0.0)
        back_buf[i] = full.astype(BF16)
    for d in far_first:

        @pl.when((z + d) % RING < DOC_SPAN)
        def _(d=d):
            back_copy(d).start()

    in_buf[z] = back_buf[z]
    forward(5)
    attend((3, 4))
    forward(6)
    attend((5, 6))
    forward(7)

    for d in far_first:
        back_copy(d).wait_recv()
    squares = jnp.zeros((TOKENS, 128), F32)
    for p in range(PAIRS):
        entering = jnp.concatenate([in_buf[2 * p], in_buf[2 * p + 1]], axis=0)
        incoming = dot(out_ref[...], entering, ((1,), (1,)))
        mixed = y_buf[p] + pair_columns(2 * LOCAL_HEADS, p) * incoming
        gate = gate_ref[:, p * 128 : (p + 1) * 128].astype(F32)
        gated = mixed * (gate / (1.0 + jnp.exp(-gate)))
        y_buf[p] = gated
        squares = squares + gated * gated
    squares_t = squares.T
    partial = squares_t[:8]
    for i in range(1, 16):
        partial = partial + squares_t[8 * i : 8 * i + 8]
    sq_buf[head] = partial
    for d in range(1, N_HEAD):
        square_copy(d).start()
    forward(8)
    attend((7, 8))
    for d in range(1, N_HEAD):
        square_copy(d).wait_recv()
    total = sq_buf[0]
    for i in range(1, N_HEAD):
        total = total + sq_buf[i]
    mean = jnp.sum(total, axis=0, keepdims=True) * (1.0 / (SSD_HEADS * HEAD_P))
    scale = jnp.broadcast_to(lax.rsqrt(mean + 1e-05), (128, TOKENS)).T
    for p in range(PAIRS):
        state_ref[:, p * 128 : (p + 1) * 128] = (
            y_buf[p] * scale * gain_ref[:, p * 128 : (p + 1) * 128]
        ).astype(BF16)

    for hop in range(DOC_SPAN):
        for copy in kv_copies(hop):
            copy.wait_send()
    for d in far_first:
        scan_copy(d).wait_send()
        back_copy(d).wait_send()
    for d in range(1, N_HEAD):
        square_copy(d).wait_send()
    carry_copy.wait_send()


def per_device(mixer_input, gate_input, input_map, output_map, step_size, decay_rate, skip_gain, norm_gain, queries, key_rows, values, segment):
    width = mixer_input.shape[1]
    vmem = pl.BlockSpec(memory_space=pltpu.VMEM)
    dma = pltpu.SemaphoreType.DMA
    out = jax.ShapeDtypeStruct((TOKENS, width), BF16)
    return pl.pallas_call(
        kernel,
        out_shape=(out, out),
        in_specs=[vmem] * 12,
        out_specs=(vmem, vmem),
        scratch_shapes=[
            pltpu.VMEM((DOC_SPAN + 1, TOKENS, TOKENS), BF16),
            pltpu.VMEM((DOC_SPAN + 1, TOKENS, HEAD_D), BF16),
            pltpu.VMEM((LOCAL_HEADS, MSG, STATE_N), BF16),
            pltpu.VMEM((RING, MSG, STATE_N), BF16),
            pltpu.VMEM((DOC_SPAN, HEAD_P, STATE_N), F32),
            pltpu.VMEM((RING, HEAD_P, STATE_N), BF16),
            pltpu.VMEM((2, MSG, STATE_N), BF16),
            pltpu.VMEM((LOCAL_HEADS, HEAD_P, STATE_N), BF16),
            pltpu.VMEM((N_HEAD, 8, TOKENS), F32),
            pltpu.VMEM((PAIRS, TOKENS, 128), F32),
            pltpu.VMEM((LOCAL_ATT, TOKENS, 2 * HEAD_D), F32),
            pltpu.VMEM((LOCAL_ATT, TOKENS, 128), F32),
            pltpu.VMEM((TOKENS, TOKENS), F32),
            pltpu.VMEM((TOKENS, 128), BF16),
            pltpu.VMEM((TOKENS, 128), F32),
            pltpu.VMEM((LOCAL_HEADS, TOKENS), F32),
            dma((DOC_SPAN,)),
            dma((DOC_SPAN,)),
            dma((DOC_SPAN,)),
            dma((DOC_SPAN,)),
            dma((RING,)),
            dma((RING,)),
            dma((1,)),
            dma((1,)),
            dma((RING,)),
            dma((RING,)),
            dma((N_HEAD,)),
            dma((N_HEAD,)),
        ],
        compiler_params=pltpu.CompilerParams(collective_id=0, has_side_effects=True, vmem_limit_bytes=40 * 2**20),
        cost_estimate=pl.CostEstimate(flops=3 * 10**9, bytes_accessed=4 * 10**6, transcendentals=6 * 10**6),
    )(
        mixer_input,
        gate_input,
        input_map,
        output_map,
        step_size,
        decay_rate[None, :],
        skip_gain[None, :],
        norm_gain[None, :],
        queries,
        key_rows,
        values,
        segment[None, :],
    )


def solution(mesh):
    in_specs = (
        P("seq", "head"),
        P("seq", "head"),
        P("seq", "head"),
        P("seq", "head"),
        P("head", "seq"),
        P("head"),
        P("head"),
        P("head"),
        P("seq", "head"),
        P("seq", "head"),
        P("seq", "head"),
        P("seq"),
    )
    out_specs = (P("seq", "head"), P("seq", "head"))
    return jax.shard_map(per_device, mesh=mesh, in_specs=in_specs, out_specs=out_specs, check_vma=False)
```

time: 624 us -> 90.5 us (0.15)
  the two profiles are of different devices: /device:TPU:505 before, /device:TPU:2 now
where the time goes in v1:
time: 90.5 us; the launch traced here: 90 us
  Pallas kernels  79.8 us (88%)
  local copies, waits for them, and re-layouts  9.47 us (10%)
    pallas_call x1, Pallas kernels, per_device(): pl.pallas_call(kernel, out_shape=(out, out), in_specs=[vmem] * 12, out_sp...  79.8 us
    unnamed x26, local copies, waits for them, and re-layouts  9.47 us

profile of v1, /device:TPU:2, one launch (start us, length us, event | category | flops | bytes accessed | tf_op | source)
XLA Modules:
  0.0 90.0 jit_solution(8016255064441550596)
XLA Ops:
  0.6 0.0 copy-start.8
  0.6 0.0 copy-start.11
  0.7 0.0 copy-start.9
  0.7 0.0 copy-start.10
  0.7 0.6 copy-done.8
  1.3 0.0 copy-done.11
  1.3 0.0 copy-done.9
  1.3 0.0 copy-done.10
  1.3 0.0 copy-start
  1.4 1.0 %copy-done = bf16[256,1024]{1,0:T(8,128)(2,1)S(1)} copy-done((bf16[256,1024]{1,0:T(8,128)(2,1)S(1)}, bf16[256,1024]{1,0:T(8,128)(2,1)}, u32[]{:S(2)}) %copy-start) | copy-done | bytes 524312
  2.4 0.0 copy-start.1
  2.4 1.0 %copy-done.1 = bf16[256,1024]{1,0:T(8,128)(2,1)S(1)} copy-done((bf16[256,1024]{1,0:T(8,128)(2,1)S(1)}, bf16[256,1024]{1,0:T(8,128)(2,1)}, u32[]{:S(2)}) %copy-start.1) | copy-done | bytes 524312
  3.4 0.0 copy-start.2
  3.4 1.0 %copy-done.2 = bf16[256,1024]{1,0:T(8,128)(2,1)S(1)} copy-done((bf16[256,1024]{1,0:T(8,128)(2,1)S(1)}, bf16[256,1024]{1,0:T(8,128)(2,1)}, u32[]{:S(2)}) %copy-start.2) | copy-done | bytes 524312
  4.5 0.0 copy-start.3
  4.5 0.8 copy-done.3
  5.3 0.0 copy-start.4
  5.3 0.8 copy-done.4
  6.2 0.8 copy-done.5
  7.0 0.8 copy-done.6
  7.8 0.7 copy-done.7
  8.6 79.8 %shard_map.131 = (bf16[256,1024]{1,0:T(8,128)(2,1)S(1)}, bf16[256,1024]{1,0:T(8,128)(2,1)S(1)}) custom-call(bf16[256,1024]{1,0:T(8,128)(2,1)S(1)} %copy-done, bf16[256,1024]{1,0:T(8,128)(2,1)S(1)} %copy-done.1, bf16[256,128]{1,0:T(8,128)(2,1)S(1)} %copy-done.3, bf16[256,128]{1,0:T(8,128)(2,1)S(1)} %copy-done.4, f32[16,256]{1,0:T(8,128)S(1)} %copy-done.7, ...), custom_call_target="tpu_custom_call" | custom-call | flops 3000000000 | bytes 4000000 | tf_op jit(solution)/shard_map/pallas_call | solution.py:369
  88.4 0.8 copy.16
  89.2 0.8 copy.17
  (3 shorter events, 0.0 us)
Async XLA Ops:
  0.6 0.7 copy-start.8
  0.6 0.7 copy-start.11
  0.7 0.7 copy-start.9
  0.7 0.7 copy-start.10
  1.3 1.0 %copy-start = (bf16[256,1024]{1,0:T(8,128)(2,1)S(1)}, bf16[256,1024]{1,0:T(8,128)(2,1)}, u32[]{:S(2)}) copy-start(bf16[256,1024]{1,0:T(8,128)(2,1)} %x_ref.1) | copy-start | bytes 1572868
  2.4 1.0 %copy-start.1 = (bf16[256,1024]{1,0:T(8,128)(2,1)S(1)}, bf16[256,1024]{1,0:T(8,128)(2,1)}, u32[]{:S(2)}) copy-start(bf16[256,1024]{1,0:T(8,128)(2,1)} %gate_ref.1) | copy-start | bytes 1572868
  3.4 1.0 %copy-start.2 = (bf16[256,1024]{1,0:T(8,128)(2,1)S(1)}, bf16[256,1024]{1,0:T(8,128)(2,1)}, u32[]{:S(2)}) copy-start(bf16[256,1024]{1,0:T(8,128)(2,1)} %q_ref.1) | copy-start | bytes 1572868
  4.5 0.8 copy-start.3
  5.3 0.8 copy-start.4
  6.2 0.8 copy-start.5
  7.0 0.8 copy-start.6
  7.8 0.7 copy-start.7

commit v2 on v1

--- a/solution.py
+++ b/solution.py
@@ -35,10 +35,11 @@
 
 
 def kernel(
-    x_ref, gate_ref, in_ref, out_ref, step_ref, decay_ref, skip_ref, gain_ref, q_ref, k_ref, v_ref, seg_ref,
+    x_hbm, gate_hbm, in_hbm, out_hbm, step_hbm, decay_hbm, skip_hbm, gain_hbm, q_hbm, k_hbm, v_hbm, seg_hbm,
     state_ref, att_ref,
+    x_ref, gate_ref, in_ref, out_ref, step_ref, decay_ref, skip_ref, gain_ref, q_ref, k_ref, v_ref, seg_ref, load_sem,
     kt_buf, v_buf, send_buf, scan_buf, local_buf, back_buf, carry_buf, in_buf, sq_buf,
-    y_buf, acc_buf, max_buf, g_buf, onehot_buf, col_buf, cum_buf,
+    y_buf, enter_buf, acc_buf, max_buf, g_buf, onehot_buf, col_buf, cum_buf,
     kt_send, kt_recv, v_send, v_recv, a_send, a_recv, c_send, c_recv, b_send, b_recv, s_send, s_recv,
 ):
     me = lax.axis_index("seq")
@@ -57,6 +58,30 @@
         pl.semaphore_signal(barrier, inc=1, device_id={"seq": other}, device_id_type=MESH)
     for d in range(1, N_HEAD):
         pl.semaphore_signal(barrier, inc=1, device_id={"head": (head + d) % N_HEAD}, device_id_type=MESH)
+
+    loads = {}
+    for i, (name, source, target) in enumerate(
+        (
+            ("step", step_hbm, step_ref),
+            ("decay", decay_hbm, decay_ref),
+            ("seg", seg_hbm, seg_ref),
+            ("in", in_hbm, in_ref),
+            ("x", x_hbm, x_ref),
+            ("k", k_hbm, k_ref),
+            ("v", v_hbm, v_ref),
+            ("out", out_hbm, out_ref),
+            ("skip", skip_hbm, skip_ref),
+            ("q", q_hbm, q_ref),
+            ("gate", gate_hbm, gate_ref),
+            ("gain", gain_hbm, gain_ref),
+        )
+    ):
+        loads[name] = pltpu.make_async_copy(source, target, load_sem.at[i])
+        loads[name].start()
+
+    def loaded(*names):
+        for name in names:
+            loads[name].wait()
 
     def kv_copies(hop):
         return (
@@ -118,6 +143,7 @@
     )
     far_first = sorted(range(1, RING), key=lambda d: -min(d, RING - d))
 
+    loaded("step", "decay", "seg")
     lane = lax.broadcasted_iota(jnp.int32, (LOCAL_HEADS, TOKENS), 1)
     diagonal = lax.broadcasted_iota(jnp.int32, (LOCAL_HEADS, LOCAL_HEADS), 0) == lax.broadcasted_iota(
         jnp.int32, (LOCAL_HEADS, LOCAL_HEADS), 1
@@ -141,6 +167,7 @@
     col_buf[...] = jnp.concatenate(
         [cum, tail, enter, jnp.zeros((128 - 3 * LOCAL_HEADS, TOKENS), F32)], axis=0
     ).T
+    loaded("in", "x")
     in_map = in_ref[...]
     in_map_t = in_map.astype(F32).T.astype(BF16)
     first_half = lax.broadcasted_iota(jnp.int32, (TOKENS, 128), 1) < HEAD_P
@@ -172,6 +199,7 @@
             )
             send_buf[h, HEAD_P:] = note.astype(BF16)
 
+    loaded("k", "v")
     kt_buf[0, :HEAD_D] = k_ref[...].astype(F32).T.astype(BF16)
     documents = lax.broadcasted_iota(jnp.int32, (16, TOKENS), 0).astype(F32)
     kt_buf[0, HEAD_D:KT_ROWS] = jnp.where(documents == seg_row, 0.0, -FAR).astype(BF16)
@@ -192,6 +220,7 @@
             if onward is not None:
                 onward.start()
 
+    loaded("out", "skip", "q", "gate", "gain")
     seg_col = jnp.broadcast_to(seg_row, (128, TOKENS)).T
     onehot_buf[...] = jnp.where(
         lax.broadcasted_iota(jnp.int32, (TOKENS, 128), 1).astype(F32) == seg_col, 1.0, 0.0
@@ -218,7 +247,10 @@
             skip = jnp.where(
                 first_half[:1], skip_ref[:, 2 * p : 2 * p + 1], skip_ref[:, 2 * p + 1 : 2 * p + 2]
             )
-            y_buf[p] = total + skip * x_pair.astype(F32)
+            gate = gate_ref[:, p * 128 : (p + 1) * 128].astype(F32)
+            opened = gate / (1.0 + jnp.exp(-gate))
+            y_buf[p] = (total + skip * x_pair.astype(F32)) * opened
+            enter_buf[p] = pair_columns(2 * LOCAL_HEADS, p) * opened
 
     def attend(hops):
         first, final = hops[0] == 0, hops[-1] == DOC_SPAN
@@ -256,99 +288,109 @@
                 max_buf[h] = best
             return 0
 
-        lax.fori_loop(0, LOCAL_ATT, one, 0)
+        lax.fori_loop(0, LOCAL_ATT, one, 0, unroll=4)
+
+    notes = []
+
+    def scan():
+        for d in far_first:
+            scan_copy(d).wait_recv()
+        state = jnp.zeros((HEAD_P, STATE_N), F32)
+        product = jnp.ones((1, STATE_N), F32)
+        last_before = None
+        for i in range(RING):
+            block = scan_buf[i].astype(F32)
+            decay = block[HEAD_P : HEAD_P + 1] + block[HEAD_P + 1 : HEAD_P + 2]
+            tag_first, tag_last = block[HEAD_P + 2 : HEAD_P + 3], block[HEAD_P + 3 : HEAD_P + 4]
+            if i >= DOC_SPAN:
+                back_buf[i] = jnp.where(tag_first == last_before, state, 0.0).astype(BF16)
+            else:
+                local_buf[i] = state
+                notes.append((product, tag_first, last_before))
+            kept = decay if i == 0 else jnp.where(tag_last == last_before, decay, 0.0)
+            state = block[:HEAD_P] + kept * state
+            product = product * decay
+            last_before = tag_last
+        carry_buf[0, :HEAD_P] = state.astype(BF16)
+        carry_buf[0, HEAD_P:] = jnp.broadcast_to(last_before, (16, STATE_N)).astype(BF16)
+        carry_copy.start()
+        for d in far_first:
+
+            @pl.when((z + d) % RING >= DOC_SPAN)
+            def _(d=d):
+                back_copy(d).start()
+
+
+    def carry():
+        carry_copy.wait_recv()
+        carried = carry_buf[1, :HEAD_P].astype(F32)
+        carried_tag = carry_buf[1, HEAD_P:].astype(F32)[:1]
+        for i, (product, tag_first, last_before) in enumerate(notes):
+            if i == 0:
+                full = jnp.where(tag_first == carried_tag, carried, 0.0)
+            else:
+                full = local_buf[i] + jnp.where(carried_tag == last_before, product, 0.0) * carried
+                full = jnp.where(tag_first == last_before, full, 0.0)
+            back_buf[i] = full.astype(BF16)
+        for d in far_first:
+
+            @pl.when((z + d) % RING < DOC_SPAN)
+            def _(d=d):
+                back_copy(d).start()
+
+        in_buf[z] = back_buf[z]
+
+    def enter_block():
+        for d in far_first:
+            back_copy(d).wait_recv()
+        squares = jnp.zeros((TOKENS, 128), F32)
+        for p in range(PAIRS):
+            entering = jnp.concatenate([in_buf[2 * p], in_buf[2 * p + 1]], axis=0)
+            incoming = dot(out_ref[...], entering, ((1,), (1,)))
+            gated = y_buf[p] + enter_buf[p] * incoming
+            y_buf[p] = gated
+            squares = squares + gated * gated
+        squares_t = squares.T
+        partial = squares_t[:8]
+        for i in range(1, 16):
+            partial = partial + squares_t[8 * i : 8 * i + 8]
+        sq_buf[head] = partial
+        for d in range(1, N_HEAD):
+            square_copy(d).start()
+
+    def normalise():
+        for d in range(1, N_HEAD):
+            square_copy(d).wait_recv()
+        total = sq_buf[0]
+        for i in range(1, N_HEAD):
+            total = total + sq_buf[i]
+        mean = jnp.sum(total, axis=0, keepdims=True) * (1.0 / (SSD_HEADS * HEAD_P))
+        scale = jnp.broadcast_to(lax.rsqrt(mean + 1e-05), (128, TOKENS)).T
+        for p in range(PAIRS):
+            state_ref[:, p * 128 : (p + 1) * 128] = (
+                y_buf[p] * scale * gain_ref[:, p * 128 : (p + 1) * 128]
+            ).astype(BF16)
+
 
     within(range(0, 4))
     forward(1)
     within(range(4, 8))
     forward(2)
     attend((0,))
+    attend((1, 2,))
+    scan()
     forward(3)
-    attend((1, 2))
-
-    for d in far_first:
-        scan_copy(d).wait_recv()
-    state = jnp.zeros((HEAD_P, STATE_N), F32)
-    product = jnp.ones((1, STATE_N), F32)
-    notes = []
-    last_before = None
-    for i in range(RING):
-        block = scan_buf[i].astype(F32)
-        decay = block[HEAD_P : HEAD_P + 1] + block[HEAD_P + 1 : HEAD_P + 2]
-        tag_first, tag_last = block[HEAD_P + 2 : HEAD_P + 3], block[HEAD_P + 3 : HEAD_P + 4]
-        if i >= DOC_SPAN:
-            back_buf[i] = jnp.where(tag_first == last_before, state, 0.0).astype(BF16)
-        else:
-            local_buf[i] = state
-            notes.append((product, tag_first, last_before))
-        kept = decay if i == 0 else jnp.where(tag_last == last_before, decay, 0.0)
-        state = block[:HEAD_P] + kept * state
-        product = product * decay
-        last_before = tag_last
-    carry_buf[0, :HEAD_P] = state.astype(BF16)
-    carry_buf[0, HEAD_P:] = jnp.broadcast_to(last_before, (16, STATE_N)).astype(BF16)
-    carry_copy.start()
-    for d in far_first:
-
-        @pl.when((z + d) % RING >= DOC_SPAN)
-        def _(d=d):
-            back_copy(d).start()
-
+    carry()
     forward(4)
-    carry_copy.wait_recv()
-    carried = carry_buf[1, :HEAD_P].astype(F32)
-    carried_tag = carry_buf[1, HEAD_P:].astype(F32)[:1]
-    for i, (product, tag_first, last_before) in enumerate(notes):
-        if i == 0:
-            full = jnp.where(tag_first == carried_tag, carried, 0.0)
-        else:
-            full = local_buf[i] + jnp.where(carried_tag == last_before, product, 0.0) * carried
-            full = jnp.where(tag_first == last_before, full, 0.0)
-        back_buf[i] = full.astype(BF16)
-    for d in far_first:
-
-        @pl.when((z + d) % RING < DOC_SPAN)
-        def _(d=d):
-            back_copy(d).start()
-
-    in_buf[z] = back_buf[z]
+    attend((3, 4,))
     forward(5)
-    attend((3, 4))
     forward(6)
-    attend((5, 6))
+    attend((5, 6,))
+    enter_block()
     forward(7)
-
-    for d in far_first:
-        back_copy(d).wait_recv()
-    squares = jnp.zeros((TOKENS, 128), F32)
-    for p in range(PAIRS):
-        entering = jnp.concatenate([in_buf[2 * p], in_buf[2 * p + 1]], axis=0)
-        incoming = dot(out_ref[...], entering, ((1,), (1,)))
-        mixed = y_buf[p] + pair_columns(2 * LOCAL_HEADS, p) * incoming
-        gate = gate_ref[:, p * 128 : (p + 1) * 128].astype(F32)
-        gated = mixed * (gate / (1.0 + jnp.exp(-gate)))
-        y_buf[p] = gated
-        squares = squares + gated * gated
-    squares_t = squares.T
-    partial = squares_t[:8]
-    for i in range(1, 16):
-        partial = partial + squares_t[8 * i : 8 * i + 8]
-    sq_buf[head] = partial
-    for d in range(1, N_HEAD):
-        square_copy(d).start()
     forward(8)
-    attend((7, 8))
-    for d in range(1, N_HEAD):
-        square_copy(d).wait_recv()
-    total = sq_buf[0]
-    for i in range(1, N_HEAD):
-        total = total + sq_buf[i]
-    mean = jnp.sum(total, axis=0, keepdims=True) * (1.0 / (SSD_HEADS * HEAD_P))
-    scale = jnp.broadcast_to(lax.rsqrt(mean + 1e-05), (128, TOKENS)).T
-    for p in range(PAIRS):
-        state_ref[:, p * 128 : (p + 1) * 128] = (
-            y_buf[p] * scale * gain_ref[:, p * 128 : (p + 1) * 128]
-        ).astype(BF16)
+    attend((7, 8,))
+    normalise()
 
     for hop in range(DOC_SPAN):
         for copy in kv_copies(hop):
@@ -366,12 +408,28 @@
     vmem = pl.BlockSpec(memory_space=pltpu.VMEM)
     dma = pltpu.SemaphoreType.DMA
     out = jax.ShapeDtypeStruct((TOKENS, width), BF16)
+    operands = (
+        mixer_input,
+        gate_input,
+        input_map,
+        output_map,
+        step_size,
+        decay_rate[None, :],
+        skip_gain[None, :],
+        norm_gain[None, :],
+        queries,
+        key_rows,
+        values,
+        segment[None, :],
+    )
     return pl.pallas_call(
         kernel,
         out_shape=(out, out),
-        in_specs=[vmem] * 12,
+        in_specs=[pl.BlockSpec(memory_space=pl.ANY)] * 12,
         out_specs=(vmem, vmem),
         scratch_shapes=[
+            *(pltpu.VMEM(a.shape, a.dtype) for a in operands),
+            dma((len(operands),)),
             pltpu.VMEM((DOC_SPAN + 1, TOKENS, TOKENS), BF16),
             pltpu.VMEM((DOC_SPAN + 1, TOKENS, HEAD_D), BF16),
             pltpu.VMEM((LOCAL_HEADS, MSG, STATE_N), BF16),
@@ -381,6 +439,7 @@
             pltpu.VMEM((2, MSG, STATE_N), BF16),
             pltpu.VMEM((LOCAL_HEADS, HEAD_P, STATE_N), BF16),
             pltpu.VMEM((N_HEAD, 8, TOKENS), F32),
+            pltpu.VMEM((PAIRS, TOKENS, 128), F32),
             pltpu.VMEM((PAIRS, TOKENS, 128), F32),
             pltpu.VMEM((LOCAL_ATT, TOKENS, 2 * HEAD_D), F32),
             pltpu.VMEM((LOCAL_ATT, TOKENS, 128), F32),
@@ -401,22 +460,9 @@
             dma((N_HEAD,)),
             dma((N_HEAD,)),
         ],
-        compiler_params=pltpu.CompilerParams(collective_id=0, has_side_effects=True, vmem_limit_bytes=40 * 2**20),
+        compiler_params=pltpu.CompilerParams(collective_id=0, has_side_effects=True, vmem_limit_bytes=56 * 2**20),
         cost_estimate=pl.CostEstimate(flops=3 * 10**9, bytes_accessed=4 * 10**6, transcendentals=6 * 10**6),
-    )(
-        mixer_input,
-        gate_input,
-        input_map,
-        output_map,
-        step_size,
-        decay_rate[None, :],
-        skip_gain[None, :],
-        norm_gain[None, :],
-        queries,
-        key_rows,
-        values,
-        segment[None, :],
-    )
+    )(*operands)
 
 
 def solution(mesh):

time: 90.5 us -> 80 us (0.88)
  the two profiles are of different devices: /device:TPU:2 before, /device:TPU:4 now
where the time goes in v2:
time: 80 us; the launch traced here: 79.8 us
  Pallas kernels  76.5 us (96%)
  local copies, waits for them, and re-layouts  2.72 us (3%)
    pallas_call x1, Pallas kernels, per_device(): pl.pallas_call(kernel, out_shape=(out, out), in_specs=[pl.BlockSpec(memor...  76.5 us
    unnamed x4, local copies, waits for them, and re-layouts  2.72 us

profile of v2, /device:TPU:4, one launch (start us, length us, event | category | flops | bytes accessed | tf_op | source)
XLA Modules:
  0.0 79.8 jit_solution(4687054076573159718)
XLA Ops:
  0.6 76.5 %shard_map.131 = (bf16[256,1024]{1,0:T(8,128)(2,1)}, bf16[256,1024]{1,0:T(8,128)(2,1)}) custom-call(bf16[256,1024]{1,0:T(8,128)(2,1)} %x_hbm.1, bf16[256,1024]{1,0:T(8,128)(2,1)} %gate_hbm.1, bf16[256,128]{1,0:T(8,128)(2,1)} %in_hbm.1, bf16[256,128]{1,0:T(8,128)(2,1)} %out_hbm.1, f32[16,256]{1,0:T(8,128)} %step_hbm.1, f32[1,16]{1,0:T(1,128)} %bitcast.6, ...), custom_call_target="tpu_custom_call" | custom-call | flops 3000000000 | bytes 4000000 | tf_op jit(solution)/shard_map/pallas_call | solution.py:425
  77.1 0.0 copy-start
  77.1 1.9 %copy.16 = bf16[256,1024]{1,0:T(8,128)(2,1)} copy(bf16[256,1024]{1,0:T(8,128)(2,1)} %get-tuple-element.4) | data formatting | bytes 1048576
  79.0 0.0 copy-done
  79.0 0.8 copy.17
Async XLA Ops:
  77.1 1.9 %copy-start = (bf16[256,1024]{1,0:T(8,128)(2,1)S(1)}, bf16[256,1024]{1,0:T(8,128)(2,1)}, u32[]{:S(2)}) copy-start(bf16[256,1024]{1,0:T(8,128)(2,1)} %get-tuple-element.5) | copy-start | bytes 1572868

commit v3 on v2

--- a/solution.py
+++ b/solution.py
@@ -16,6 +16,7 @@
 TOKENS = 256
 N_SEQ = 64
 RING = 16
+RELAYED = (7, 8)
 N_HEAD = 8
 LOCAL_HEADS = SSD_HEADS // N_HEAD
 LOCAL_ATT = ATT_HEADS // N_HEAD
@@ -38,9 +39,9 @@
     x_hbm, gate_hbm, in_hbm, out_hbm, step_hbm, decay_hbm, skip_hbm, gain_hbm, q_hbm, k_hbm, v_hbm, seg_hbm,
     state_ref, att_ref,
     x_ref, gate_ref, in_ref, out_ref, step_ref, decay_ref, skip_ref, gain_ref, q_ref, k_ref, v_ref, seg_ref, load_sem,
-    kt_buf, v_buf, send_buf, scan_buf, local_buf, back_buf, carry_buf, in_buf, sq_buf,
+    kt_buf, v_buf, send_buf, scan_buf, note_buf, relay_buf, local_buf, back_buf, carry_buf, in_buf, sq_buf,
     y_buf, enter_buf, acc_buf, max_buf, g_buf, onehot_buf, col_buf, cum_buf,
-    kt_send, kt_recv, v_send, v_recv, a_send, a_recv, c_send, c_recv, b_send, b_recv, s_send, s_recv,
+    kv_send, kv_recv, n_send, n_recv, r_send, r_recv, f_send, a_send, a_recv, c_send, c_recv, b_send, b_recv, s_send, s_recv,
 ):
     me = lax.axis_index("seq")
     head = lax.axis_index("head")
@@ -84,24 +85,24 @@
             loads[name].wait()
 
     def kv_copies(hop):
-        return (
+        return [
             pltpu.make_async_remote_copy(
-                src_ref=kt_buf.at[hop, pl.ds(0, KT_ROWS)],
-                dst_ref=kt_buf.at[hop + 1, pl.ds(0, KT_ROWS)],
-                send_sem=kt_send.at[hop],
-                recv_sem=kt_recv.at[hop],
+                src_ref=buf.at[hop, pl.ds(start, size)],
+                dst_ref=buf.at[hop + 1, pl.ds(start, size)],
+                send_sem=kv_send.at[hop, i],
+                recv_sem=kv_recv.at[hop, i],
                 device_id={"seq": succ},
                 device_id_type=MESH,
-            ),
-            pltpu.make_async_remote_copy(
-                src_ref=v_buf.at[hop],
-                dst_ref=v_buf.at[hop + 1],
-                send_sem=v_send.at[hop],
-                recv_sem=v_recv.at[hop],
-                device_id={"seq": succ},
-                device_id_type=MESH,
-            ),
-        )
+            )
+            for i, (buf, start, size) in enumerate(
+                (
+                    (kt_buf, 0, KT_ROWS - 64),
+                    (kt_buf, KT_ROWS - 64, 64),
+                    (v_buf, 0, TOKENS // 2),
+                    (v_buf, TOKENS // 2, TOKENS // 2),
+                )
+            )
+        ]
 
     def scan_copy(d):
         return pltpu.make_async_remote_copy(
@@ -133,6 +134,41 @@
             device_id_type=MESH,
         )
 
+    def note_copy(d):
+        return pltpu.make_async_remote_copy(
+            src_ref=note_buf.at[z],
+            dst_ref=note_buf.at[z],
+            send_sem=n_send.at[d],
+            recv_sem=n_recv.at[d],
+            device_id={"seq": ring(d)},
+            device_id_type=MESH,
+        )
+
+    def relay_out(phase, far):
+        return pltpu.make_async_remote_copy(
+            src_ref=(send_buf, back_buf)[phase].at[(z + far) % RING],
+            dst_ref=relay_buf.at[phase, far - RELAYED[0]],
+            send_sem=r_send.at[phase, far - RELAYED[0]],
+            recv_sem=r_recv.at[phase, far - RELAYED[0]],
+            device_id={"seq": ring(RING - RING // 4)},
+            device_id_type=MESH,
+        )
+
+    def relay_on(phase, far):
+        return pltpu.make_async_remote_copy(
+            src_ref=relay_buf.at[phase, far - RELAYED[0]],
+            dst_ref=(scan_buf, in_buf)[phase].at[(z + RING // 4) % RING],
+            send_sem=f_send.at[phase, far - RELAYED[0]],
+            recv_sem=(a_recv, b_recv)[phase].at[far],
+            device_id={"seq": ring(far + RING // 4)},
+            device_id_type=MESH,
+        )
+
+    def relay(phase):
+        for far in RELAYED:
+            relay_out(phase, far).wait_recv()
+            relay_on(phase, far).start()
+
     carry_copy = pltpu.make_async_remote_copy(
         src_ref=carry_buf.at[0],
         dst_ref=carry_buf.at[1],
@@ -141,7 +177,7 @@
         device_id={"seq": below},
         device_id_type=MESH,
     )
-    far_first = sorted(range(1, RING), key=lambda d: -min(d, RING - d))
+    far_first = sorted((d for d in range(1, RING) if d not in RELAYED), key=lambda d: -min(d, RING - d))
 
     loaded("step", "decay", "seg")
     lane = lax.broadcasted_iota(jnp.int32, (LOCAL_HEADS, TOKENS), 1)
@@ -177,27 +213,18 @@
         b = jnp.broadcast_to(col_buf[:, base + 2 * p + 1 : base + 2 * p + 2], (TOKENS, 128))
         return jnp.where(first_half, a, b)
 
-    block_decay = jnp.broadcast_to(jnp.exp2(-last_cum), (LOCAL_HEADS, 128))
-    decay_hi = block_decay.astype(BF16).astype(F32)
-    decay_lo = block_decay - decay_hi
-    note_row = lax.broadcasted_iota(jnp.int32, (16, 128), 0)
-    tags = jnp.where(
-        note_row == 2,
-        jnp.broadcast_to(seg_first, (16, 128)),
-        jnp.where(note_row == 3, jnp.broadcast_to(seg_last, (16, 128)), 0.0),
+    note_lane = lax.broadcasted_iota(jnp.int32, (1, 128), 1)
+    note_buf[z] = jnp.where(
+        note_lane < LOCAL_HEADS,
+        jnp.exp2(-col_buf[TOKENS - 1 :, :]),
+        jnp.where(note_lane == LOCAL_HEADS, seg_first, seg_last),
     )
     for p in range(PAIRS):
         weighted = (x_ref[:, p * 128 : (p + 1) * 128].astype(F32) * pair_columns(LOCAL_HEADS, p)).astype(BF16)
         end_state = dot(in_map_t, weighted).T.astype(BF16)
         for half in range(2):
             h = 2 * p + half
-            send_buf[h, :HEAD_P] = end_state[half * HEAD_P : (half + 1) * HEAD_P]
-            note = jnp.where(
-                note_row == 0,
-                jnp.broadcast_to(decay_hi[h : h + 1], (16, 128)),
-                jnp.where(note_row == 1, jnp.broadcast_to(decay_lo[h : h + 1], (16, 128)), tags),
-            )
-            send_buf[h, HEAD_P:] = note.astype(BF16)
+            send_buf[h] = end_state[half * HEAD_P : (half + 1) * HEAD_P]
 
     loaded("k", "v")
     kt_buf[0, :HEAD_D] = k_ref[...].astype(F32).T.astype(BF16)
@@ -208,14 +235,18 @@
         kt_buf[hop, KT_ROWS:] = jnp.zeros((TOKENS - KT_ROWS, TOKENS), BF16)
 
     pl.semaphore_wait(barrier, RING - 1 + 4 + N_HEAD - 1)
+    for far in RELAYED:
+        relay_out(0, far).start()
     for d in far_first:
         scan_copy(d).start()
+    for d in range(1, RING):
+        note_copy(d).start()
     for copy in kv_copies(0):
         copy.start()
     scan_buf[z] = send_buf[z]
 
     def forward(hop):
-        for copy, onward in zip(kv_copies(hop - 1), kv_copies(hop) if hop < DOC_SPAN else (None, None)):
+        for copy, onward in zip(kv_copies(hop - 1), kv_copies(hop) if hop < DOC_SPAN else [None] * 4):
             copy.wait_recv()
             if onward is not None:
                 onward.start()
@@ -295,25 +326,42 @@
     def scan():
         for d in far_first:
             scan_copy(d).wait_recv()
+        for far in RELAYED:
+            relay_on(0, far).wait_recv()
+        for d in range(1, RING):
+            note_copy(d).wait_recv()
+        all_notes = jnp.concatenate([note_buf[i] for i in range(RING)], axis=0)
+        decays = jnp.sum(
+            jnp.where(lax.broadcasted_iota(jnp.int32, (RING, 128), 1) == z, all_notes, 0.0), axis=1, keepdims=True
+        )
+        decays = jnp.broadcast_to(decays, (RING, STATE_N))
+        firsts = jnp.broadcast_to(all_notes[:, LOCAL_HEADS : LOCAL_HEADS + 1], (RING, STATE_N))
+        lasts = jnp.broadcast_to(all_notes[:, LOCAL_HEADS + 1 : LOCAL_HEADS + 2], (RING, STATE_N))
         state = jnp.zeros((HEAD_P, STATE_N), F32)
         product = jnp.ones((1, STATE_N), F32)
         last_before = None
         for i in range(RING):
             block = scan_buf[i].astype(F32)
-            decay = block[HEAD_P : HEAD_P + 1] + block[HEAD_P + 1 : HEAD_P + 2]
-            tag_first, tag_last = block[HEAD_P + 2 : HEAD_P + 3], block[HEAD_P + 3 : HEAD_P + 4]
+            decay, tag_first, tag_last = decays[i : i + 1], firsts[i : i + 1], lasts[i : i + 1]
             if i >= DOC_SPAN:
                 back_buf[i] = jnp.where(tag_first == last_before, state, 0.0).astype(BF16)
             else:
                 local_buf[i] = state
                 notes.append((product, tag_first, last_before))
             kept = decay if i == 0 else jnp.where(tag_last == last_before, decay, 0.0)
-            state = block[:HEAD_P] + kept * state
+            state = block + kept * state
             product = product * decay
             last_before = tag_last
         carry_buf[0, :HEAD_P] = state.astype(BF16)
         carry_buf[0, HEAD_P:] = jnp.broadcast_to(last_before, (16, STATE_N)).astype(BF16)
         carry_copy.start()
+
+        for far in RELAYED:
+
+            @pl.when((z + far) % RING >= DOC_SPAN)
+            def _(far=far):
+                relay_out(1, far).start()
+
         for d in far_first:
 
             @pl.when((z + d) % RING >= DOC_SPAN)
@@ -332,6 +380,13 @@
                 full = local_buf[i] + jnp.where(carried_tag == last_before, product, 0.0) * carried
                 full = jnp.where(tag_first == last_before, full, 0.0)
             back_buf[i] = full.astype(BF16)
+
+        for far in RELAYED:
+
+            @pl.when((z + far) % RING < DOC_SPAN)
+            def _(far=far):
+                relay_out(1, far).start()
+
         for d in far_first:
 
             @pl.when((z + d) % RING < DOC_SPAN)
@@ -343,6 +398,8 @@
     def enter_block():
         for d in far_first:
             back_copy(d).wait_recv()
+        for far in RELAYED:
+            relay_on(1, far).wait_recv()
         squares = jnp.zeros((TOKENS, 128), F32)
         for p in range(PAIRS):
             entering = jnp.concatenate([in_buf[2 * p], in_buf[2 * p + 1]], axis=0)
@@ -372,24 +429,28 @@
             ).astype(BF16)
 
 
-    within(range(0, 4))
     forward(1)
-    within(range(4, 8))
+    relay(0)
+    within(range(0, 8))
     forward(2)
     attend((0,))
-    attend((1, 2,))
+    attend((1,))
     scan()
     forward(3)
+    attend((2,))
     carry()
     forward(4)
-    attend((3, 4,))
+    relay(1)
+    attend((3, 4))
     forward(5)
+    attend((5,))
     forward(6)
-    attend((5, 6,))
+    attend((6,))
     enter_block()
     forward(7)
+    attend((7,))
     forward(8)
-    attend((7, 8,))
+    attend((8,))
     normalise()
 
     for hop in range(DOC_SPAN):
@@ -401,6 +462,12 @@
     for d in range(1, N_HEAD):
         square_copy(d).wait_send()
     carry_copy.wait_send()
+    for phase in range(2):
+        for far in RELAYED:
+            relay_out(phase, far).wait_send()
+            relay_on(phase, far).wait_send()
+    for d in range(1, RING):
+        note_copy(d).wait_send()
 
 
 def per_device(mixer_input, gate_input, input_map, output_map, step_size, decay_rate, skip_gain, norm_gain, queries, key_rows, values, segment):
@@ -432,8 +499,10 @@
             dma((len(operands),)),
             pltpu.VMEM((DOC_SPAN + 1, TOKENS, TOKENS), BF16),
             pltpu.VMEM((DOC_SPAN + 1, TOKENS, HEAD_D), BF16),
-            pltpu.VMEM((LOCAL_HEADS, MSG, STATE_N), BF16),
-            pltpu.VMEM((RING, MSG, STATE_N), BF16),
+            pltpu.VMEM((LOCAL_HEADS, HEAD_P, STATE_N), BF16),
+            pltpu.VMEM((RING, HEAD_P, STATE_N), BF16),
+            pltpu.VMEM((RING, 1, 128), F32),
+            pltpu.VMEM((2, len(RELAYED), HEAD_P, STATE_N), BF16),
             pltpu.VMEM((DOC_SPAN, HEAD_P, STATE_N), F32),
             pltpu.VMEM((RING, HEAD_P, STATE_N), BF16),
             pltpu.VMEM((2, MSG, STATE_N), BF16),
@@ -447,10 +516,13 @@
             pltpu.VMEM((TOKENS, 128), BF16),
             pltpu.VMEM((TOKENS, 128), F32),
             pltpu.VMEM((LOCAL_HEADS, TOKENS), F32),
-            dma((DOC_SPAN,)),
-            dma((DOC_SPAN,)),
-            dma((DOC_SPAN,)),
-            dma((DOC_SPAN,)),
+            dma((DOC_SPAN, 4)),
+            dma((DOC_SPAN, 4)),
+            dma((RING,)),
+            dma((RING,)),
+            dma((2, len(RELAYED))),
+            dma((2, len(RELAYED))),
+            dma((2, len(RELAYED))),
             dma((RING,)),
             dma((RING,)),
             dma((1,)),

time: 80 us -> 70.1 us (0.88)
  the two profiles are of different devices: /device:TPU:4 before, /device:TPU:1 now
where the time goes in v3:
time: 70.1 us; the launch traced here: 69.9 us
  Pallas kernels  66.5 us (95%)
  local copies, waits for them, and re-layouts  2.72 us (4%)
    pallas_call x1, Pallas kernels, per_device(): pl.pallas_call(kernel, out_shape=(out, out), in_specs=[pl.BlockSpec(memor...  66.5 us
    unnamed x4, local copies, waits for them, and re-layouts  2.72 us

profile of v3, /device:TPU:1, one launch (start us, length us, event | category | flops | bytes accessed | tf_op | source)
XLA Modules:
  0.0 69.9 jit_solution(2150276346308994481)
XLA Ops:
  0.6 66.5 %shard_map.131 = (bf16[256,1024]{1,0:T(8,128)(2,1)}, bf16[256,1024]{1,0:T(8,128)(2,1)}) custom-call(bf16[256,1024]{1,0:T(8,128)(2,1)} %x_hbm.1, bf16[256,1024]{1,0:T(8,128)(2,1)} %gate_hbm.1, bf16[256,128]{1,0:T(8,128)(2,1)} %in_hbm.1, bf16[256,128]{1,0:T(8,128)(2,1)} %out_hbm.1, f32[16,256]{1,0:T(8,128)} %step_hbm.1, f32[1,16]{1,0:T(1,128)} %bitcast.6, ...), custom_call_target="tpu_custom_call" | custom-call | flops 3000000000 | bytes 4000000 | tf_op jit(solution)/shard_map/pallas_call | solution.py:492
  67.1 0.0 copy-start
  67.2 1.9 %copy.16 = bf16[256,1024]{1,0:T(8,128)(2,1)} copy(bf16[256,1024]{1,0:T(8,128)(2,1)} %get-tuple-element.4) | data formatting | bytes 1048576
  69.1 0.0 copy-done
  69.1 0.8 %copy.17 = bf16[256,1024]{1,0:T(8,128)(2,1)} copy(bf16[256,1024]{1,0:T(8,128)(2,1)S(1)} %copy-done) | data formatting | bytes 1048576
Async XLA Ops:
  67.1 1.9 %copy-start = (bf16[256,1024]{1,0:T(8,128)(2,1)S(1)}, bf16[256,1024]{1,0:T(8,128)(2,1)}, u32[]{:S(2)}) copy-start(bf16[256,1024]{1,0:T(8,128)(2,1)} %get-tuple-element.5) | copy-start | bytes 1572868

commit v4 on v3

--- a/solution.py
+++ b/solution.py
@@ -16,7 +16,7 @@
 TOKENS = 256
 N_SEQ = 64
 RING = 16
-RELAYED = (7, 8)
+RELAYED = ((7, 8), (7, 8))
 N_HEAD = 8
 LOCAL_HEADS = SSD_HEADS // N_HEAD
 LOCAL_ATT = ATT_HEADS // N_HEAD
@@ -39,7 +39,7 @@
     x_hbm, gate_hbm, in_hbm, out_hbm, step_hbm, decay_hbm, skip_hbm, gain_hbm, q_hbm, k_hbm, v_hbm, seg_hbm,
     state_ref, att_ref,
     x_ref, gate_ref, in_ref, out_ref, step_ref, decay_ref, skip_ref, gain_ref, q_ref, k_ref, v_ref, seg_ref, load_sem,
-    kt_buf, v_buf, send_buf, scan_buf, note_buf, relay_buf, local_buf, back_buf, carry_buf, in_buf, sq_buf,
+    kt_buf, v_buf, tag_buf, send_buf, scan_buf, note_buf, relay_buf, local_buf, back_buf, carry_buf, in_buf, sq_buf,
     y_buf, enter_buf, acc_buf, max_buf, g_buf, onehot_buf, col_buf, cum_buf,
     kv_send, kv_recv, n_send, n_recv, r_send, r_recv, f_send, a_send, a_recv, c_send, c_recv, b_send, b_recv, s_send, s_recv,
 ):
@@ -87,19 +87,18 @@
     def kv_copies(hop):
         return [
             pltpu.make_async_remote_copy(
-                src_ref=buf.at[hop, pl.ds(start, size)],
-                dst_ref=buf.at[hop + 1, pl.ds(start, size)],
+                src_ref=source,
+                dst_ref=target,
                 send_sem=kv_send.at[hop, i],
                 recv_sem=kv_recv.at[hop, i],
                 device_id={"seq": succ},
                 device_id_type=MESH,
             )
-            for i, (buf, start, size) in enumerate(
+            for i, (source, target) in enumerate(
                 (
-                    (kt_buf, 0, KT_ROWS - 64),
-                    (kt_buf, KT_ROWS - 64, 64),
-                    (v_buf, 0, TOKENS // 2),
-                    (v_buf, TOKENS // 2, TOKENS // 2),
+                    (kt_buf.at[hop, pl.ds(0, HEAD_D)], kt_buf.at[hop + 1, pl.ds(0, HEAD_D)]),
+                    (v_buf.at[hop], v_buf.at[hop + 1]),
+                    (tag_buf.at[hop], tag_buf.at[hop + 1]),
                 )
             )
         ]
@@ -147,25 +146,25 @@
     def relay_out(phase, far):
         return pltpu.make_async_remote_copy(
             src_ref=(send_buf, back_buf)[phase].at[(z + far) % RING],
-            dst_ref=relay_buf.at[phase, far - RELAYED[0]],
-            send_sem=r_send.at[phase, far - RELAYED[0]],
-            recv_sem=r_recv.at[phase, far - RELAYED[0]],
+            dst_ref=relay_buf.at[phase, far - 7],
+            send_sem=r_send.at[phase, far - 7],
+            recv_sem=r_recv.at[phase, far - 7],
             device_id={"seq": ring(RING - RING // 4)},
             device_id_type=MESH,
         )
 
     def relay_on(phase, far):
         return pltpu.make_async_remote_copy(
-            src_ref=relay_buf.at[phase, far - RELAYED[0]],
+            src_ref=relay_buf.at[phase, far - 7],
             dst_ref=(scan_buf, in_buf)[phase].at[(z + RING // 4) % RING],
-            send_sem=f_send.at[phase, far - RELAYED[0]],
+            send_sem=f_send.at[phase, far - 7],
             recv_sem=(a_recv, b_recv)[phase].at[far],
             device_id={"seq": ring(far + RING // 4)},
             device_id_type=MESH,
         )
 
     def relay(phase):
-        for far in RELAYED:
+        for far in RELAYED[phase]:
             relay_out(phase, far).wait_recv()
             relay_on(phase, far).start()
 
@@ -177,7 +176,10 @@
         device_id={"seq": below},
         device_id_type=MESH,
     )
-    far_first = sorted((d for d in range(1, RING) if d not in RELAYED), key=lambda d: -min(d, RING - d))
+    direct = [
+        sorted((d for d in range(1, RING) if d not in RELAYED[phase]), key=lambda d: -min(d, RING - d))
+        for phase in range(2)
+    ]
 
     loaded("step", "decay", "seg")
     lane = lax.broadcasted_iota(jnp.int32, (LOCAL_HEADS, TOKENS), 1)
@@ -229,15 +231,20 @@
     loaded("k", "v")
     kt_buf[0, :HEAD_D] = k_ref[...].astype(F32).T.astype(BF16)
     documents = lax.broadcasted_iota(jnp.int32, (16, TOKENS), 0).astype(F32)
-    kt_buf[0, HEAD_D:KT_ROWS] = jnp.where(documents == seg_row, 0.0, -FAR).astype(BF16)
+    tag_buf[0] = seg_row
+
+    def mask_rows(hop):
+        kt_buf[hop, HEAD_D:KT_ROWS] = jnp.where(documents == tag_buf[hop], 0.0, -FAR).astype(BF16)
+
+    mask_rows(0)
     v_buf[0] = v_ref[...]
     for hop in range(DOC_SPAN + 1):
         kt_buf[hop, KT_ROWS:] = jnp.zeros((TOKENS - KT_ROWS, TOKENS), BF16)
 
     pl.semaphore_wait(barrier, RING - 1 + 4 + N_HEAD - 1)
-    for far in RELAYED:
+    for far in RELAYED[0]:
         relay_out(0, far).start()
-    for d in far_first:
+    for d in direct[0]:
         scan_copy(d).start()
     for d in range(1, RING):
         note_copy(d).start()
@@ -246,10 +253,11 @@
     scan_buf[z] = send_buf[z]
 
     def forward(hop):
-        for copy, onward in zip(kv_copies(hop - 1), kv_copies(hop) if hop < DOC_SPAN else [None] * 4):
+        for copy, onward in zip(kv_copies(hop - 1), kv_copies(hop) if hop < DOC_SPAN else [None] * 3):
             copy.wait_recv()
             if onward is not None:
                 onward.start()
+        mask_rows(hop)
 
     loaded("out", "skip", "q", "gate", "gain")
     seg_col = jnp.broadcast_to(seg_row, (128, TOKENS)).T
@@ -324,9 +332,9 @@
     notes = []
 
     def scan():
-        for d in far_first:
+        for d in direct[0]:
             scan_copy(d).wait_recv()
-        for far in RELAYED:
+        for far in RELAYED[0]:
             relay_on(0, far).wait_recv()
         for d in range(1, RING):
             note_copy(d).wait_recv()
@@ -356,13 +364,13 @@
         carry_buf[0, HEAD_P:] = jnp.broadcast_to(last_before, (16, STATE_N)).astype(BF16)
         carry_copy.start()
 
-        for far in RELAYED:
+        for far in RELAYED[1]:
 
             @pl.when((z + far) % RING >= DOC_SPAN)
             def _(far=far):
                 relay_out(1, far).start()
 
-        for d in far_first:
+        for d in direct[1]:
 
             @pl.when((z + d) % RING >= DOC_SPAN)
             def _(d=d):
@@ -381,13 +389,13 @@
                 full = jnp.where(tag_first == last_before, full, 0.0)
             back_buf[i] = full.astype(BF16)
 
-        for far in RELAYED:
+        for far in RELAYED[1]:
 
             @pl.when((z + far) % RING < DOC_SPAN)
             def _(far=far):
                 relay_out(1, far).start()
 
-        for d in far_first:
+        for d in direct[1]:
 
             @pl.when((z + d) % RING < DOC_SPAN)
             def _(d=d):
@@ -396,9 +404,9 @@
         in_buf[z] = back_buf[z]
 
     def enter_block():
-        for d in far_first:
+        for d in direct[1]:
             back_copy(d).wait_recv()
-        for far in RELAYED:
+        for far in RELAYED[1]:
             relay_on(1, far).wait_recv()
         squares = jnp.zeros((TOKENS, 128), F32)
         for p in range(PAIRS):
@@ -433,22 +441,19 @@
     relay(0)
     within(range(0, 8))
     forward(2)
-    attend((0,))
-    attend((1,))
+    attend((0, 1))
     scan()
     forward(3)
-    attend((2,))
     carry()
     forward(4)
     relay(1)
-    attend((3, 4))
+    attend((2, 3))
     forward(5)
-    attend((5,))
+    attend((4, 5))
     forward(6)
-    attend((6,))
     enter_block()
     forward(7)
-    attend((7,))
+    attend((6, 7))
     forward(8)
     attend((8,))
     normalise()
@@ -456,14 +461,15 @@
     for hop in range(DOC_SPAN):
         for copy in kv_copies(hop):
             copy.wait_send()
-    for d in far_first:
+    for d in direct[0]:
         scan_copy(d).wait_send()
+    for d in direct[1]:
         back_copy(d).wait_send()
     for d in range(1, N_HEAD):
         square_copy(d).wait_send()
     carry_copy.wait_send()
     for phase in range(2):
-        for far in RELAYED:
+        for far in RELAYED[phase]:
             relay_out(phase, far).wait_send()
             relay_on(phase, far).wait_send()
     for d in range(1, RING):
@@ -499,10 +505,11 @@
             dma((len(operands),)),
             pltpu.VMEM((DOC_SPAN + 1, TOKENS, TOKENS), BF16),
             pltpu.VMEM((DOC_SPAN + 1, TOKENS, HEAD_D), BF16),
+            pltpu.VMEM((DOC_SPAN + 1, 1, TOKENS), F32),
             pltpu.VMEM((LOCAL_HEADS, HEAD_P, STATE_N), BF16),
             pltpu.VMEM((RING, HEAD_P, STATE_N), BF16),
             pltpu.VMEM((RING, 1, 128), F32),
-            pltpu.VMEM((2, len(RELAYED), HEAD_P, STATE_N), BF16),
+            pltpu.VMEM((2, 2, HEAD_P, STATE_N), BF16),
             pltpu.VMEM((DOC_SPAN, HEAD_P, STATE_N), F32),
             pltpu.VMEM((RING, HEAD_P, STATE_N), BF16),
             pltpu.VMEM((2, MSG, STATE_N), BF16),
@@ -516,13 +523,13 @@
             pltpu.VMEM((TOKENS, 128), BF16),
             pltpu.VMEM((TOKENS, 128), F32),
             pltpu.VMEM((LOCAL_HEADS, TOKENS), F32),
-            dma((DOC_SPAN, 4)),
-            dma((DOC_SPAN, 4)),
+            dma((DOC_SPAN, 3)),
+            dma((DOC_SPAN, 3)),
             dma((RING,)),
             dma((RING,)),
-            dma((2, len(RELAYED))),
-            dma((2, len(RELAYED))),
-            dma((2, len(RELAYED))),
+            dma((2, 2)),
+            dma((2, 2)),
+            dma((2, 2)),
             dma((RING,)),
             dma((RING,)),
             dma((1,)),

time: 70.1 us -> 69.2 us (0.987); the launches traced: 69.9 us -> 67.8 us
  Pallas kernels: 66.5 us -> 64.4 us
    pallas_call x1, Pallas kernels: 66.5 us -> 64.4 us  [per_device(): pl.pallas_call(kernel, out_shape=(out, out), in_specs=[pl.BlockSpec(memor...]
where the time goes in v4:
time: 69.2 us; the launch traced here: 67.8 us
  Pallas kernels  64.4 us (93%)
  local copies, waits for them, and re-layouts  2.72 us (4%)
    pallas_call x1, Pallas kernels, per_device(): pl.pallas_call(kernel, out_shape=(out, out), in_specs=[pl.BlockSpec(memor...  64.4 us
    unnamed x4, local copies, waits for them, and re-layouts  2.72 us

profile of v4, /device:TPU:1, one launch (start us, length us, event | category | flops | bytes accessed | tf_op | source)
XLA Modules:
  0.0 67.8 jit_solution(2263306928585891077)
XLA Ops:
  0.6 64.4 %shard_map.131 = (bf16[256,1024]{1,0:T(8,128)(2,1)}, bf16[256,1024]{1,0:T(8,128)(2,1)}) custom-call(bf16[256,1024]{1,0:T(8,128)(2,1)} %x_hbm.1, bf16[256,1024]{1,0:T(8,128)(2,1)} %gate_hbm.1, bf16[256,128]{1,0:T(8,128)(2,1)} %in_hbm.1, bf16[256,128]{1,0:T(8,128)(2,1)} %out_hbm.1, f32[16,256]{1,0:T(8,128)} %step_hbm.1, f32[1,16]{1,0:T(1,128)} %bitcast.6, ...), custom_call_target="tpu_custom_call" | custom-call | flops 3000000000 | bytes 4000000 | tf_op jit(solution)/shard_map/pallas_call | solution.py:498
  65.1 0.0 copy-start
  65.1 1.9 %copy.16 = bf16[256,1024]{1,0:T(8,128)(2,1)} copy(bf16[256,1024]{1,0:T(8,128)(2,1)} %get-tuple-element.4) | data formatting | bytes 1048576
  67.0 0.0 copy-done
  67.0 0.8 %copy.17 = bf16[256,1024]{1,0:T(8,128)(2,1)} copy(bf16[256,1024]{1,0:T(8,128)(2,1)S(1)} %copy-done) | data formatting | bytes 1048576
Async XLA Ops:
  65.1 1.9 %copy-start = (bf16[256,1024]{1,0:T(8,128)(2,1)S(1)}, bf16[256,1024]{1,0:T(8,128)(2,1)}, u32[]{:S(2)}) copy-start(bf16[256,1024]{1,0:T(8,128)(2,1)} %get-tuple-element.5) | copy-start | bytes 1572868

commit v5 on v4

--- a/solution.py
+++ b/solution.py
@@ -327,7 +327,7 @@
                 max_buf[h] = best
             return 0
 
-        lax.fori_loop(0, LOCAL_ATT, one, 0, unroll=4)
+        lax.fori_loop(0, LOCAL_ATT, one, 0, unroll=8)
 
     notes = []
 

time: 69.2 us -> 69.1 us (level)
  no operation moved by 1% of the time
where the time goes in v5:
time: 69.1 us; the launch traced here: 67.9 us
  Pallas kernels  64.5 us (93%)
  local copies, waits for them, and re-layouts  2.72 us (4%)
    pallas_call x1, Pallas kernels, per_device(): pl.pallas_call(kernel, out_shape=(out, out), in_specs=[pl.BlockSpec(memor...  64.5 us
    unnamed x4, local copies, waits for them, and re-layouts  2.72 us

profile of v5, /device:TPU:1, one launch (start us, length us, event | category | flops | bytes accessed | tf_op | source)
XLA Modules:
  0.0 67.9 jit_solution(10275099820246466826)
XLA Ops:
  0.6 64.5 %shard_map.131 = (bf16[256,1024]{1,0:T(8,128)(2,1)}, bf16[256,1024]{1,0:T(8,128)(2,1)}) custom-call(bf16[256,1024]{1,0:T(8,128)(2,1)} %x_hbm.1, bf16[256,1024]{1,0:T(8,128)(2,1)} %gate_hbm.1, bf16[256,128]{1,0:T(8,128)(2,1)} %in_hbm.1, bf16[256,128]{1,0:T(8,128)(2,1)} %out_hbm.1, f32[16,256]{1,0:T(8,128)} %step_hbm.1, f32[1,16]{1,0:T(1,128)} %bitcast.6, ...), custom_call_target="tpu_custom_call" | custom-call | flops 3000000000 | bytes 4000000 | tf_op jit(solution)/shard_map/pallas_call | solution.py:498
  65.2 0.0 copy-start
  65.2 1.9 %copy.16 = bf16[256,1024]{1,0:T(8,128)(2,1)} copy(bf16[256,1024]{1,0:T(8,128)(2,1)} %get-tuple-element.4) | data formatting | bytes 1048576
  67.1 0.0 copy-done
  67.1 0.8 %copy.17 = bf16[256,1024]{1,0:T(8,128)(2,1)} copy(bf16[256,1024]{1,0:T(8,128)(2,1)S(1)} %copy-done) | data formatting | bytes 1048576
Async XLA Ops:
  65.2 1.9 %copy-start = (bf16[256,1024]{1,0:T(8,128)(2,1)S(1)}, bf16[256,1024]{1,0:T(8,128)(2,1)}, u32[]{:S(2)}) copy-start(bf16[256,1024]{1,0:T(8,128)(2,1)} %get-tuple-element.5) | copy-start | bytes 1572868
